TPU v7x, 32 devices: a whole 2x2x4 slice. The times are simulated.
32 devices in a mesh: row: 4 (over y, core), col: 8 (over z, x).
Axes of the slice: x: 2, y: 2, z: 4, core: 2. Of those that a mesh axis runs over, the one named last changes fastest.
Arguments:
- ancestor: bfloat16 [32, 32, 256, 256], P('row', 'col'), may hold values from -6 to 6
- tile_mask: int32 [32, 32], P('row', 'col'), may hold values 0 or 1
- member_one: int32 [32], replicated, may hold values 0 or 1
- member_two: int32 [32], replicated, may hold values 0 or 1
- factor_one: bfloat16 [32, 256, 256], P('row'), may hold values from -0.0625 to 0.0625
- factor_two: bfloat16 [32, 256, 256], P('row'), may hold values from -0.0625 to 0.0625
- link_block: bfloat16 [256, 256], replicated, may hold values from -0.375 to 0.375
- inverse_one: float32 [256, 256], replicated, may hold values from -6 to 6
- inverse_two: float32 [256, 256], replicated, may hold values from -6 to 6
Outputs:
- column_one: bfloat16 [32, 256, 256], P(('row', 'col'))
- column_two: bfloat16 [32, 256, 256], P(('row', 'col'))
- diag_one: bfloat16 [256, 256], replicated
- cross_block: bfloat16 [256, 256], replicated
- diag_two: bfloat16 [256, 256], replicated
All inputs are finite; a program needn't handle non-finite values. No bound on the sum of `tile_mask` on one device may be relied on, other than what follows from the above.
Results may differ from a plain program's by a relative error of at most 0.01.
Values may be sent and summed in bfloat16 or wider, within the bound.
No kernel may reach another device: no remote copies, remote signals or barrier semaphores. Data moves between devices by JAX's collectives and lax.ppermute only.
A program may use at most 128 MiB of HBM per device.

v0:
```python
import functools

import jax
import jax.numpy as jnp
from jax import lax
from jax.experimental import pallas as pl
from jax.experimental.pallas import tpu as pltpu
from jax.sharding import PartitionSpec as P

F32, BF16 = jnp.float32, jnp.bfloat16
BOTH = ("row", "col")


def product_kernel(cols, n_fac, ids, marks, flags, *refs):
    anc, column = refs[:2]
    factors, (out, sums), acc = refs[2 : 2 + n_fac], refs[2 + n_fac : 4 + n_fac], refs[-1]
    step = pl.program_id(0)
    s = ids[step]

    @pl.when(step == 0)
    def _():
        sums[...] = jnp.zeros_like(sums)

    acc[...] = jnp.zeros_like(acc)
    for j in range(cols):

        @pl.when(marks[s * cols + j] > 0)
        def _(j=j):
            acc[...] += jnp.dot(anc[0, j], column[j], preferred_element_type=F32)

    low = acc[...].astype(BF16)
    out[0] = low
    for k in range(n_fac):

        @pl.when(flags[s * n_fac + k] > 0)
        def _(k=k):
            sums[k] += lax.dot_general(
                factors[k][0], low, (((0,), (0,)), ((), ())), preferred_element_type=F32
            )


def products(ids, marks, flags, ancestor, column, factors):
    rows, cols, tile, _ = ancestor.shape
    n, n_fac = ids.shape[0], len(factors)
    block = lambda i, ids, *_: (ids[i], 0, 0)
    return pl.pallas_call(
        functools.partial(product_kernel, cols, n_fac),
        out_shape=(
            jax.ShapeDtypeStruct((n, tile, tile), BF16),
            jax.ShapeDtypeStruct((n_fac, tile, tile), F32),
        ),
        grid_spec=pltpu.PrefetchScalarGridSpec(
            num_scalar_prefetch=3,
            grid=(n,),
            in_specs=[
                pl.BlockSpec((1, cols, tile, tile), lambda i, ids, *_: (ids[i], 0, 0, 0)),
                pl.BlockSpec((cols, tile, tile), lambda i, *_: (0, 0, 0)),
            ]
            + [pl.BlockSpec((1, tile, tile), block)] * n_fac,
            out_specs=[
                pl.BlockSpec((1, tile, tile), lambda i, *_: (i, 0, 0)),
                pl.BlockSpec((n_fac, tile, tile), lambda i, *_: (0, 0, 0)),
            ],
            scratch_shapes=[pltpu.VMEM((tile, tile), F32)],
        ),
        compiler_params=pltpu.CompilerParams(vmem_limit_bytes=32 << 20),
        cost_estimate=pl.CostEstimate(
            flops=2 * n * (cols + n_fac) * tile**3,
            bytes_accessed=2 * n * (cols + n_fac + 1) * tile**2,
            transcendentals=0,
        ),
    )(ids, marks, flags, ancestor, column, *factors)


def shards(
    ancestor,
    tile_mask,
    member_one,
    member_two,
    factor_one,
    factor_two,
    link_block,
    inverse_one,
    inverse_two,
):
    nrow, ncol = lax.axis_size("row"), lax.axis_size("col")
    row, col = lax.axis_index("row"), lax.axis_index("col")
    rows, cols, tile = ancestor.shape[0], ancestor.shape[1], ancestor.shape[-1]
    group = ncol // nrow
    bits = ncol.bit_length() - 1
    owner = col // group
    at = lambda r, c: r * ncol + c

    def spread(factor):
        have = piece = lax.dynamic_slice_in_dim(factor, col % group * cols, cols, 0)
        for k in range(2, nrow, 2):
            perm = [(at(c // group, c), at((c // group + k) % nrow, c)) for c in range(ncol)]
            have = jnp.where((row - owner) % nrow == k, lax.ppermute(piece, BOTH, perm), have)
        perm = [
            (at(2 * y + c // group % 2, c), at(2 * y + 1 - c // group % 2, c))
            for y in range(nrow // 2)
            for c in range(ncol)
        ]
        return jnp.where((row - owner) % 2 == 0, have, lax.ppermute(have, BOTH, perm))

    def halves(array, bit):
        split = array.reshape(array.shape[0] // 2, 2, tile, tile)
        mine = (col >> bit) & 1
        pick = lambda b: lax.dynamic_slice_in_dim(split, b, 1, 1)[:, 0]
        return pick(1 - mine), pick(mine)

    def swap(array, bit):
        perm = [(at(r, c), at(r, c ^ (1 << bit))) for r in range(nrow) for c in range(ncol)]
        return lax.ppermute(array, BOTH, perm)

    flags_one = lax.dynamic_slice_in_dim(member_one, row * rows, rows, 0)
    flags_two = lax.dynamic_slice_in_dim(member_two, row * rows, rows, 0)
    marks = [
        (tile_mask * lax.dynamic_slice_in_dim(m, col * cols, cols, 0)[None]).reshape(-1)
        for m in (member_one, member_two)
    ]
    flags = [jnp.stack([flags_one, flags_one * flags_two], 1).reshape(-1), flags_two]
    ids = jnp.arange(rows // 2, dtype=jnp.int32) * 2
    leave, stay = ids + (1 - col % 2), ids + col % 2

    totals, contracted = [], []
    factors = [(factor_one, factor_two), (factor_two,)]
    for k, factor in enumerate((factor_one, factor_two)):
        column = spread(factor)
        args = (marks[k], flags[k], ancestor, column, factors[k])
        away, part_a = products(leave, *args)
        got = swap(away, 0)
        keep, part_b = products(stay, *args)
        contracted.append(part_a + part_b)
        for bit in range(1, bits):
            summed = keep.astype(F32) + got.astype(F32)
            away, keep = halves(summed, bit)
            got = swap(away.astype(BF16), bit)
        totals.append((keep.astype(F32) + got.astype(F32))[0])

    parts = jnp.concatenate(contracted).astype(BF16)
    high = parts.shape[0] * tile // nrow
    part = lax.all_to_all(parts.reshape(nrow, high, tile), "row", 0, 0)
    part = part.astype(F32).sum(0).astype(BF16)
    part = lax.all_to_all(part.reshape(ncol, high // ncol, tile), "col", 0, 0)
    part = part.astype(F32).sum(0).astype(BF16)
    part = lax.all_to_all(jnp.broadcast_to(part, (ncol,) + part.shape), "col", 0, 0)
    part = part.reshape(high, tile)
    part = lax.all_to_all(jnp.broadcast_to(part, (nrow,) + part.shape), "row", 0, 0)
    sum_one, sum_cross, sum_two = part.reshape(parts.shape)

    mine_one = lax.dynamic_index_in_dim(flags_one, col, keepdims=False).astype(F32)
    mine_two = lax.dynamic_index_in_dim(flags_two, col, keepdims=False).astype(F32)
    column_one = (-mine_one * totals[0]).astype(BF16)
    y_two = mine_two * (totals[1] + jnp.dot(column_one, link_block, preferred_element_type=F32))
    column_two = (-y_two).astype(BF16)

    diag_one = (inverse_one + sum_one.astype(F32)).astype(BF16)
    cross_block = (
        sum_cross.astype(F32).T - jnp.dot(diag_one, link_block, preferred_element_type=F32)
    ).astype(BF16)
    diag_two = (
        inverse_two
        + sum_two.astype(F32)
        - jnp.dot(sum_cross, link_block, preferred_element_type=F32)
        - jnp.dot(link_block.T, cross_block, preferred_element_type=F32)
    ).astype(BF16)
    return (column_one[None], column_two[None], diag_one, cross_block, diag_two)


def solution(mesh):
    in_specs = (
        P("row", "col", None, None),
        P("row", "col"),
        P(),
        P(),
        P("row", None, None),
        P("row", None, None),
        P(),
        P(),
        P(),
    )
    out_specs = (P(("row", "col"), None, None), P(("row", "col"), None, None), P(), P(), P())
    return jax.shard_map(shards, mesh=mesh, in_specs=in_specs, out_specs=out_specs, check_vma=False)
```

profile of v0, /device:TPU:0, one launch (start us, length us, event | category | flops | bytes accessed | tf_op | source)
XLA Modules:
  0.0 98.7 jit_solution(6756404765016423460)
XLA Ops:
  0.7 1.2 %constant_dynamic-slice_fusion = bf16[4,256,256]{2,1,0:T(8,128)(2,1)S(1)} fusion(bf16[8,256,256]{2,1,0:T(8,128)(2,1)} %refs_2_.7, s32[]{:T(128)S(6)} %select_n.99), kind=kLoop, calls=%fused_computation.37 | loop fusion | bytes 1048580 | tf_op jit(solution)/shard_map/dynamic_slice | solution.py:95
  1.9 4.9 %collective-permute-start.5 = (bf16[4,256,256]{2,1,0:T(8,128)(2,1)S(1)}, bf16[4,256,256]{2,1,0:T(8,128)(2,1)S(1)}, u32[]{:S(2)}, u32[]{:S(2)}) collective-permute-start(bf16[4,256,256]{2,1,0:T(8,128)(2,1)S(1)} %constant_dynamic-slice_fusion), channel_id=1, source_target_pairs={{0,16},{1,17},{10,26},{11,27},{20,4},{21,5},{30,14},{31,15}} | collective-permute-start | bytes 1572872 | tf_op jit(solution)/shard_map/ppermute | solution.py:98
  6.8 1.1 %constant_dynamic-slice_fusion.1 = bf16[4,256,256]{2,1,0:T(8,128)(2,1)S(1)} fusion(bf16[8,256,256]{2,1,0:T(8,128)(2,1)} %refs_2_.5, s32[]{:T(128)S(6)} %select_n.99), kind=kLoop, calls=%fused_computation.38 | loop fusion | bytes 1048580 | tf_op jit(solution)/shard_map/dynamic_slice | solution.py:95
  7.8 2.1 %collective-permute-start = (bf16[4,256,256]{2,1,0:T(8,128)(2,1)S(1)}, bf16[4,256,256]{2,1,0:T(8,128)(2,1)}, u32[]{:S(2)}, u32[]{:S(2)}) collective-permute-start(bf16[4,256,256]{2,1,0:T(8,128)(2,1)S(1)} %constant_dynamic-slice_fusion.1), channel_id=1, source_target_pairs={{0,16},{1,17},{10,26},{11,27},{20,4},{21,5},{30,14},{31,15}} | collective-permute-start | bytes 1572872 | tf_op jit(solution)/shard_map/ppermute | solution.py:98
  13.4 1.1 %broadcast_select_fusion = bf16[4,256,256]{2,1,0:T(8,128)(2,1)S(1)} fusion(bf16[4,256,256]{2,1,0:T(8,128)(2,1)S(1)} %collective-permute-done.5, pred[]{:T(512)S(6)} %eq.18, bf16[8,256,256]{2,1,0:T(8,128)(2,1)} %refs_2_.7, s32[]{:T(128)S(6)} %select_n.99), kind=kLoop, calls=%fused_computation.13 | loop fusion | flops 262144 | bytes 1572869 | tf_op jit(solution)/shard_map/jit(_where)/select_n | solution.py:98
  14.5 1.3 %collective-permute-start.6 = (bf16[4,256,256]{2,1,0:T(8,128)(2,1)S(1)}, bf16[4,256,256]{2,1,0:T(8,128)(2,1)S(1)}, u32[]{:S(2)}, u32[]{:S(2)}) collective-permute-start(bf16[4,256,256]{2,1,0:T(8,128)(2,1)S(1)} %broadcast_select_fusion), channel_id=1, source_target_pairs={{0,8},{1,9},{10,2},{11,3},{4,12},{5,13},{14,6},{15,7},{16,24},{17,... | collective-permute-start | bytes 1572872 | tf_op jit(solution)/shard_map/ppermute | solution.py:104
  15.9 3.2 %collective-permute-done = bf16[4,256,256]{2,1,0:T(8,128)(2,1)} collective-permute-done((bf16[4,256,256]{2,1,0:T(8,128)(2,1)S(1)}, bf16[4,256,256]{2,1,0:T(8,128)(2,1)}, u32[]{:S(2)}, u32[]{:S(2)}) %collective-permute-start) | collective-permute-done | bytes 524320 | tf_op jit(solution)/shard_map/ppermute | solution.py:98
  19.0 1.1 %broadcast_select_fusion.1 = bf16[4,256,256]{2,1,0:T(8,128)(2,1)S(1)} fusion(bf16[4,256,256]{2,1,0:T(8,128)(2,1)} %collective-permute-done, pred[]{:T(512)S(6)} %eq.18, bf16[8,256,256]{2,1,0:T(8,128)(2,1)} %refs_2_.5, s32[]{:T(128)S(6)} %select_n.99), kind=kLoop, calls=%fused_computation.14 | loop fusion | flops 262144 | bytes 1572869 | tf_op jit(solution)/shard_map/jit(_where)/select_n | solution.py:98
  20.1 2.1 %collective-permute-start.1 = (bf16[4,256,256]{2,1,0:T(8,128)(2,1)S(1)}, bf16[4,256,256]{2,1,0:T(8,128)(2,1)}, u32[]{:S(2)}, u32[]{:S(2)}) collective-permute-start(bf16[4,256,256]{2,1,0:T(8,128)(2,1)S(1)} %broadcast_select_fusion.1), channel_id=1, source_target_pairs={{0,8},{1,9},{10,2},{11,3},{4,12},{5,13},{14,6},{15,7},{16,24},{17,... | collective-permute-start | bytes 1572872 | tf_op jit(solution)/shard_map/ppermute | solution.py:104
  22.8 2.2 %copy-done.1 = bf16[8,4,256,256]{3,2,1,0:T(8,128)(2,1)S(1)} copy-done((bf16[8,4,256,256]{3,2,1,0:T(8,128)(2,1)S(1)}, bf16[8,4,256,256]{3,2,1,0:T(8,128)(2,1)}, u32[]{:S(2)}) %copy-start.1) | copy-done | bytes 4194328
  25.0 2.6 %shard_map.131 = (bf16[4,256,256]{2,1,0:T(8,128)(2,1)S(1)}, f32[1,256,256]{2,1,0:T(8,128)S(1)}) custom-call(s32[4]{0:T(128)S(1)} %fusion.15.ids, s32[32]{0:T(128)S(1)} %reshape.68.marks, s32[8]{0:T(128)S(1)} %get-tuple-element.27.flags, bf16[8,4,256,256]{3,2,1,0:T(8,128)(2,1)S(1)} %copy-done.1, bf16[4,256,256]{2,1,0:T(8,128)(2,1)S(1)} %broadcast_select_fusion.2.refs_1_, ...), custom_call_target="tpu_custom_call" | custom-call | flops 671088640 | bytes 3145728 | tf_op jit(solution)/shard_map/pallas_call | solution.py:46
  27.6 2.9 %shard_map.130 = (bf16[4,256,256]{2,1,0:T(8,128)(2,1)S(1)}, f32[1,256,256]{2,1,0:T(8,128)S(1)}) custom-call(s32[4]{0:T(128)S(1)} %fusion.16.ids, s32[32]{0:T(128)S(1)} %reshape.68.marks, s32[8]{0:T(128)S(1)} %get-tuple-element.27.flags, bf16[8,4,256,256]{3,2,1,0:T(8,128)(2,1)S(1)} %copy-done.2, bf16[4,256,256]{2,1,0:T(8,128)(2,1)S(1)} %broadcast_select_fusion.2.refs_1_, ...), custom_call_target="tpu_custom_call" | custom-call | flops 671088640 | bytes 3145728 | tf_op jit(solution)/shard_map/pallas_call | solution.py:46
  30.6 2.5 %shard_map.128 = (bf16[4,256,256]{2,1,0:T(8,128)(2,1)S(1)}, f32[2,256,256]{2,1,0:T(8,128)S(1)}) custom-call(s32[4]{0:T(128)S(1)} %fusion.16.ids, s32[32]{0:T(128)S(1)} %reshape.65.marks, s32[16]{0:T(128)S(1)} %reshape.66.flags, bf16[8,4,256,256]{3,2,1,0:T(8,128)(2,1)S(1)} %copy-done.2, bf16[4,256,256]{2,1,0:T(8,128)(2,1)S(1)} %broadcast_select_fusion.3.refs_1_, ...), custom_call_target="tpu_custom_call" | custom-call | flops 805306368 | bytes 3670016 | tf_op jit(solution)/shard_map/pallas_call | solution.py:46
  33.2 2.5 %shard_map.129 = (bf16[4,256,256]{2,1,0:T(8,128)(2,1)S(1)}, f32[2,256,256]{2,1,0:T(8,128)S(1)}) custom-call(s32[4]{0:T(128)S(1)} %fusion.15.ids, s32[32]{0:T(128)S(1)} %reshape.65.marks, s32[16]{0:T(128)S(1)} %reshape.66.flags, bf16[8,4,256,256]{3,2,1,0:T(8,128)(2,1)S(1)} %copy-done.2, bf16[4,256,256]{2,1,0:T(8,128)(2,1)S(1)} %broadcast_select_fusion.3.refs_1_, ...), custom_call_target="tpu_custom_call" | custom-call | flops 805306368 | bytes 3670016 | tf_op jit(solution)/shard_map/pallas_call | solution.py:46
  35.7 2.5 %collective-permute-start.2 = (bf16[4,256,256]{2,1,0:T(8,128)(2,1)S(1)}, bf16[4,256,256]{2,1,0:T(8,128)(2,1)}, u32[]{:S(2)}, u32[]{:S(2)}) collective-permute-start(bf16[4,256,256]{2,1,0:T(8,128)(2,1)S(1)} %get-tuple-element.14), channel_id=1, source_target_pairs={{0,1},{1,0},{2,3},{3,2},{4,5},{5,4},{6,7},{7,6},{8,9},{9,8},{10,11... | collective-permute-start | bytes 1572872 | tf_op jit(solution)/shard_map/ppermute | solution.py:114
  38.3 10.4 %all_to_all.20 = bf16[4,192,256]{2,1,0:T(8,128)(2,1)S(1)} all-to-all(bf16[4,192,256]{2,1,0:T(8,128)(2,1)S(1)} %bitcast.77), channel_id=1, replica_groups=mesh['row'=4,'col'=8] {'row'}, dimensions={0} | all-to-all | bytes 786432 | tf_op jit(solution)/shard_map/all_to_all | solution.py:143
  49.4 5.9 %all-to-all-start.1 = ((bf16[8,24,256]{2,1,0:T(8,128)(2,1)}), bf16[8,24,256]{2,1,0:T(8,128)(2,1)S(1)}, u32[]{:S(2)}, u32[]{:S(2)}) async-start(bf16[8,24,256]{2,1,0:T(8,128)(2,1)} %bitcast.14), calls=%async_computation.1 | async-start | bytes 196608 | tf_op jit(solution)/shard_map/all_to_all | solution.py:145
  55.3 2.0 %collective-permute-start.7 = (bf16[4,256,256]{2,1,0:T(8,128)(2,1)S(1)}, bf16[4,256,256]{2,1,0:T(8,128)(2,1)}, u32[]{:S(2)}, u32[]{:S(2)}) collective-permute-start(bf16[4,256,256]{2,1,0:T(8,128)(2,1)S(1)} %get-tuple-element.16), channel_id=1, source_target_pairs={{0,1},{1,0},{2,3},{3,2},{4,5},{5,4},{6,7},{7,6},{8,9},{9,8},{10,11... | collective-permute-start | bytes 1572872 | tf_op jit(solution)/shard_map/ppermute | solution.py:114
  59.8 2.7 %all-to-all-done.1 = bf16[8,24,256]{2,1,0:T(8,128)(2,1)S(1)} async-done(((bf16[8,24,256]{2,1,0:T(8,128)(2,1)}), bf16[8,24,256]{2,1,0:T(8,128)(2,1)S(1)}, u32[]{:S(2)}, u32[]{:S(2)}) %all-to-all-start.1) | async-done | bytes 98336 | tf_op jit(solution)/shard_map/all_to_all | solution.py:145
  63.2 3.4 %all-to-all-start.2 = ((bf16[8,24,256]{2,1,0:T(8,128)(2,1)}), bf16[8,24,256]{2,1,0:T(8,128)(2,1)S(1)}, u32[]{:S(2)}, u32[]{:S(2)}) async-start(bf16[8,24,256]{2,1,0:T(8,128)(2,1)} %broadcast_in_dim.13), calls=%async_computation.2 | async-start | bytes 196608 | tf_op jit(solution)/shard_map/all_to_all | solution.py:147
  66.6 1.1 %convert_add_fusion.1 = f32[4,256,256]{2,1,0:T(8,128)S(1)} fusion(bf16[4,256,256]{2,1,0:T(8,128)(2,1)} %collective-permute-done.2, bf16[4,256,256]{2,1,0:T(8,128)(2,1)S(1)} %get-tuple-element.13), kind=kLoop, calls=%fused_computation.7 | loop fusion | flops 786432 | bytes 2097152 | tf_op jit(solution)/shard_map/add | solution.py:136
  68.5 1.9 %collective-permute-start.3 = (bf16[2,256,256]{2,1,0:T(8,128)(2,1)}, bf16[2,256,256]{2,1,0:T(8,128)(2,1)}, u32[]{:S(2)}, u32[]{:S(2)}) collective-permute-start(bf16[2,256,256]{2,1,0:T(8,128)(2,1)} %fusion.3), channel_id=1, source_target_pairs={{0,2},{1,3},{2,0},{3,1},{4,6},{5,7},{6,4},{7,5},{8,10},{9,11},{10,... | collective-permute-start | bytes 786440 | tf_op jit(solution)/shard_map/ppermute | solution.py:114
  70.4 1.1 %convert_add_fusion = f32[4,256,256]{2,1,0:T(8,128)S(1)} fusion(bf16[4,256,256]{2,1,0:T(8,128)(2,1)} %collective-permute-done.7, bf16[4,256,256]{2,1,0:T(8,128)(2,1)S(1)} %get-tuple-element.15), kind=kLoop, calls=%fused_computation.6 | loop fusion | flops 786432 | bytes 2097152 | tf_op jit(solution)/shard_map/add | solution.py:136
  72.3 1.3 %collective-permute-start.8 = (bf16[2,256,256]{2,1,0:T(8,128)(2,1)}, bf16[2,256,256]{2,1,0:T(8,128)(2,1)}, u32[]{:S(2)}, u32[]{:S(2)}) collective-permute-start(bf16[2,256,256]{2,1,0:T(8,128)(2,1)} %fusion.4), channel_id=1, source_target_pairs={{0,2},{1,3},{2,0},{3,1},{4,6},{5,7},{6,4},{7,5},{8,10},{9,11},{10,... | collective-permute-start | bytes 786440 | tf_op jit(solution)/shard_map/ppermute | solution.py:114
  75.1 3.5 %all-to-all-start.3 = ((bf16[4,192,256]{2,1,0:T(8,128)(2,1)}), bf16[4,192,256]{2,1,0:T(8,128)(2,1)S(1)}, u32[]{:S(2)}, u32[]{:S(2)}) async-start(bf16[4,192,256]{2,1,0:T(8,128)(2,1)} %broadcast_in_dim.14), calls=%async_computation.3 | async-start | bytes 786432 | tf_op jit(solution)/shard_map/all_to_all | solution.py:149
  78.5 1.0 %bitcast_add_fusion.1 = f32[2,256,256]{2,1,0:T(8,128)S(1)} fusion(bf16[2,256,256]{2,1,0:T(8,128)(2,1)} %collective-permute-done.3, f32[2,2,256,256]{3,2,1,0:T(8,128)S(1)} %bitcast.71, s32[]{:T(128)S(6)} %select_n.102), kind=kLoop, calls=%fused_computation.11 | loop fusion | flops 262144 | bytes 1310724 | tf_op jit(solution)/shard_map/add | solution.py:136
  79.6 2.3 %collective-permute-start.4 = (bf16[1,256,256]{2,1,0:T(8,128)(2,1)S(1)}, bf16[1,256,256]{2,1,0:T(8,128)(2,1)S(1)}, u32[]{:S(2)}, u32[]{:S(2)}) collective-permute-start(bf16[1,256,256]{2,1,0:T(8,128)(2,1)S(1)} %dynamic-slice_convert_fusion.1), channel_id=1, source_target_pairs={{0,4},{1,5},{2,6},{3,7},{4,0},{5,1},{6,2},{7,3},{8,12},{9,13},{10,... | collective-permute-start | bytes 393224 | tf_op jit(solution)/shard_map/ppermute | solution.py:114
  81.9 1.0 %bitcast_add_fusion = f32[2,256,256]{2,1,0:T(8,128)S(1)} fusion(bf16[2,256,256]{2,1,0:T(8,128)(2,1)} %collective-permute-done.8, f32[2,2,256,256]{3,2,1,0:T(8,128)S(1)} %bitcast.73, s32[]{:T(128)S(6)} %select_n.102), kind=kLoop, calls=%fused_computation.10 | loop fusion | flops 262144 | bytes 1310724 | tf_op jit(solution)/shard_map/add | solution.py:136
  83.0 2.2 %collective-permute-start.9 = (bf16[1,256,256]{2,1,0:T(8,128)(2,1)S(1)}, bf16[1,256,256]{2,1,0:T(8,128)(2,1)S(1)}, u32[]{:S(2)}, u32[]{:S(2)}) collective-permute-start(bf16[1,256,256]{2,1,0:T(8,128)(2,1)S(1)} %dynamic-slice_convert_fusion), channel_id=1, source_target_pairs={{0,4},{1,5},{2,6},{3,7},{4,0},{5,1},{6,2},{7,3},{8,12},{9,13},{10,... | collective-permute-start | bytes 393224 | tf_op jit(solution)/shard_map/ppermute | solution.py:114
  85.1 6.6 %collective-permute-done.4 = bf16[1,256,256]{2,1,0:T(8,128)(2,1)S(1)} collective-permute-done((bf16[1,256,256]{2,1,0:T(8,128)(2,1)S(1)}, bf16[1,256,256]{2,1,0:T(8,128)(2,1)S(1)}, u32[]{:S(2)}, u32[]{:S(2)}) %collective-permute-start.4) | collective-permute-done | bytes 131104 | tf_op jit(solution)/shard_map/ppermute | solution.py:114
  91.8 2.7 %collective-permute-done.9 = bf16[1,256,256]{2,1,0:T(8,128)(2,1)S(1)} collective-permute-done((bf16[1,256,256]{2,1,0:T(8,128)(2,1)S(1)}, bf16[1,256,256]{2,1,0:T(8,128)(2,1)S(1)}, u32[]{:S(2)}, u32[]{:S(2)}) %collective-permute-start.9) | collective-permute-done | bytes 131104 | tf_op jit(solution)/shard_map/ppermute | solution.py:114
  96.9 1.8 %fusion.2 = bf16[256,256]{1,0:T(8,128)(2,1)} fusion(f32[256,256]{1,0:T(8,128)S(1)} %convolution_bitcast_fusion, bf16[256,256]{1,0:T(8,128)(2,1)S(1)} %copy-done, f32[256,256]{1,0:T(8,128)} %param.17, bf16[3,256,256]{2,1,0:T(8,128)(2,1)S(1)} %bitcast.76), kind=kOutput, calls=%fused_computation.5 | convolution fusion | flops 33882112 | bytes 1048576 | tf_op jit(solution)/shard_map/dot_general | solution.py:165
  (63 shorter events, 12.3 us)
Async XLA Ops:
  0.6 93.9 %copy-start = (bf16[256,256]{1,0:T(8,128)(2,1)S(1)}, bf16[256,256]{1,0:T(8,128)(2,1)}, u32[]{:S(2)}) copy-start(bf16[256,256]{1,0:T(8,128)(2,1)} %param.15) | copy-start | bytes 393220
  0.6 22.2 %copy-start.3 = (bf16[8,256,256]{2,1,0:T(8,128)(2,1)S(1)}, bf16[8,256,256]{2,1,0:T(8,128)(2,1)}, u32[]{:S(2)}) copy-start(bf16[8,256,256]{2,1,0:T(8,128)(2,1)} %refs_2_.7) | copy-start | bytes 3145732
  1.9 11.6 %collective-permute-start.5 = (bf16[4,256,256]{2,1,0:T(8,128)(2,1)S(1)}, bf16[4,256,256]{2,1,0:T(8,128)(2,1)S(1)}, u32[]{:S(2)}, u32[]{:S(2)}) collective-permute-start(bf16[4,256,256]{2,1,0:T(8,128)(2,1)S(1)} %constant_dynamic-slice_fusion), channel_id=1, source_target_pairs={{0,16},{1,17},{10,26},{11,27},{20,4},{21,5},{30,14},{31,15}} | collective-permute-start | bytes 1572872 | tf_op jit(solution)/shard_map/ppermute | solution.py:98
  7.8 11.2 %collective-permute-start = (bf16[4,256,256]{2,1,0:T(8,128)(2,1)S(1)}, bf16[4,256,256]{2,1,0:T(8,128)(2,1)}, u32[]{:S(2)}, u32[]{:S(2)}) collective-permute-start(bf16[4,256,256]{2,1,0:T(8,128)(2,1)S(1)} %constant_dynamic-slice_fusion.1), channel_id=1, source_target_pairs={{0,16},{1,17},{10,26},{11,27},{20,4},{21,5},{30,14},{31,15}} | collective-permute-start | bytes 1572872 | tf_op jit(solution)/shard_map/ppermute | solution.py:98
  14.5 8.2 %collective-permute-start.6 = (bf16[4,256,256]{2,1,0:T(8,128)(2,1)S(1)}, bf16[4,256,256]{2,1,0:T(8,128)(2,1)S(1)}, u32[]{:S(2)}, u32[]{:S(2)}) collective-permute-start(bf16[4,256,256]{2,1,0:T(8,128)(2,1)S(1)} %broadcast_select_fusion), channel_id=1, source_target_pairs={{0,8},{1,9},{10,2},{11,3},{4,12},{5,13},{14,6},{15,7},{16,24},{17,... | collective-permute-start | bytes 1572872 | tf_op jit(solution)/shard_map/ppermute | solution.py:104
  20.1 10.4 %collective-permute-start.1 = (bf16[4,256,256]{2,1,0:T(8,128)(2,1)S(1)}, bf16[4,256,256]{2,1,0:T(8,128)(2,1)}, u32[]{:S(2)}, u32[]{:S(2)}) collective-permute-start(bf16[4,256,256]{2,1,0:T(8,128)(2,1)S(1)} %broadcast_select_fusion.1), channel_id=1, source_target_pairs={{0,8},{1,9},{10,2},{11,3},{4,12},{5,13},{14,6},{15,7},{16,24},{17,... | collective-permute-start | bytes 1572872 | tf_op jit(solution)/shard_map/ppermute | solution.py:104
  22.8 2.2 %copy-start.1 = (bf16[8,4,256,256]{3,2,1,0:T(8,128)(2,1)S(1)}, bf16[8,4,256,256]{3,2,1,0:T(8,128)(2,1)}, u32[]{:S(2)}) copy-start(bf16[8,4,256,256]{3,2,1,0:T(8,128)(2,1)} %refs_0_.7) | copy-start | bytes 12582916
  25.0 2.6 %copy-start.2 = (bf16[8,4,256,256]{3,2,1,0:T(8,128)(2,1)S(1)}, bf16[8,4,256,256]{3,2,1,0:T(8,128)(2,1)}, u32[]{:S(2)}) copy-start(bf16[8,4,256,256]{3,2,1,0:T(8,128)(2,1)} %refs_0_.7) | copy-start | bytes 12582916
  27.6 3.0 %copy-start.4 = (bf16[8,256,256]{2,1,0:T(8,128)(2,1)S(1)}, bf16[8,256,256]{2,1,0:T(8,128)(2,1)}, u32[]{:S(2)}) copy-start(bf16[8,256,256]{2,1,0:T(8,128)(2,1)} %refs_2_.5) | copy-start | bytes 3145732
  33.1 24.2 %copy-start.8 = (s32[32]{0:T(128)S(1)}, s32[32]{0:T(128)}, u32[]{:S(2)}) copy-start(s32[32]{0:T(128)} %param.12) | copy-start | bytes 388
  33.2 24.8 %copy-start.9 = (s32[32]{0:T(128)S(1)}, s32[32]{0:T(128)}, u32[]{:S(2)}) copy-start(s32[32]{0:T(128)} %param.11) | copy-start | bytes 388
  35.7 30.9 %collective-permute-start.2 = (bf16[4,256,256]{2,1,0:T(8,128)(2,1)S(1)}, bf16[4,256,256]{2,1,0:T(8,128)(2,1)}, u32[]{:S(2)}, u32[]{:S(2)}) collective-permute-start(bf16[4,256,256]{2,1,0:T(8,128)(2,1)S(1)} %get-tuple-element.14), channel_id=1, source_target_pairs={{0,1},{1,0},{2,3},{3,2},{4,5},{5,4},{6,7},{7,6},{8,9},{9,8},{10,11... | collective-permute-start | bytes 1572872 | tf_op jit(solution)/shard_map/ppermute | solution.py:114
  49.4 13.1 %all-to-all-start.1 = ((bf16[8,24,256]{2,1,0:T(8,128)(2,1)}), bf16[8,24,256]{2,1,0:T(8,128)(2,1)S(1)}, u32[]{:S(2)}, u32[]{:S(2)}) async-start(bf16[8,24,256]{2,1,0:T(8,128)(2,1)} %bitcast.14), calls=%async_computation.1 | async-start | bytes 196608 | tf_op jit(solution)/shard_map/all_to_all | solution.py:145
  55.3 15.1 %collective-permute-start.7 = (bf16[4,256,256]{2,1,0:T(8,128)(2,1)S(1)}, bf16[4,256,256]{2,1,0:T(8,128)(2,1)}, u32[]{:S(2)}, u32[]{:S(2)}) collective-permute-start(bf16[4,256,256]{2,1,0:T(8,128)(2,1)S(1)} %get-tuple-element.16), channel_id=1, source_target_pairs={{0,1},{1,0},{2,3},{3,2},{4,5},{5,4},{6,7},{7,6},{8,9},{9,8},{10,11... | collective-permute-start | bytes 1572872 | tf_op jit(solution)/shard_map/ppermute | solution.py:114
  63.2 11.1 %all-to-all-start.2 = ((bf16[8,24,256]{2,1,0:T(8,128)(2,1)}), bf16[8,24,256]{2,1,0:T(8,128)(2,1)S(1)}, u32[]{:S(2)}, u32[]{:S(2)}) async-start(bf16[8,24,256]{2,1,0:T(8,128)(2,1)} %broadcast_in_dim.13), calls=%async_computation.2 | async-start | bytes 196608 | tf_op jit(solution)/shard_map/all_to_all | solution.py:147
  68.5 10.0 %collective-permute-start.3 = (bf16[2,256,256]{2,1,0:T(8,128)(2,1)}, bf16[2,256,256]{2,1,0:T(8,128)(2,1)}, u32[]{:S(2)}, u32[]{:S(2)}) collective-permute-start(bf16[2,256,256]{2,1,0:T(8,128)(2,1)} %fusion.3), channel_id=1, source_target_pairs={{0,2},{1,3},{2,0},{3,1},{4,6},{5,7},{6,4},{7,5},{8,10},{9,11},{10,... | collective-permute-start | bytes 786440 | tf_op jit(solution)/shard_map/ppermute | solution.py:114
  72.3 9.6 %collective-permute-start.8 = (bf16[2,256,256]{2,1,0:T(8,128)(2,1)}, bf16[2,256,256]{2,1,0:T(8,128)(2,1)}, u32[]{:S(2)}, u32[]{:S(2)}) collective-permute-start(bf16[2,256,256]{2,1,0:T(8,128)(2,1)} %fusion.4), channel_id=1, source_target_pairs={{0,2},{1,3},{2,0},{3,1},{4,6},{5,7},{6,4},{7,5},{8,10},{9,11},{10,... | collective-permute-start | bytes 786440 | tf_op jit(solution)/shard_map/ppermute | solution.py:114
  75.1 20.3 %all-to-all-start.3 = ((bf16[4,192,256]{2,1,0:T(8,128)(2,1)}), bf16[4,192,256]{2,1,0:T(8,128)(2,1)S(1)}, u32[]{:S(2)}, u32[]{:S(2)}) async-start(bf16[4,192,256]{2,1,0:T(8,128)(2,1)} %broadcast_in_dim.14), calls=%async_computation.3 | async-start | bytes 786432 | tf_op jit(solution)/shard_map/all_to_all | solution.py:149
  79.6 12.1 %collective-permute-start.4 = (bf16[1,256,256]{2,1,0:T(8,128)(2,1)S(1)}, bf16[1,256,256]{2,1,0:T(8,128)(2,1)S(1)}, u32[]{:S(2)}, u32[]{:S(2)}) collective-permute-start(bf16[1,256,256]{2,1,0:T(8,128)(2,1)S(1)} %dynamic-slice_convert_fusion.1), channel_id=1, source_target_pairs={{0,4},{1,5},{2,6},{3,7},{4,0},{5,1},{6,2},{7,3},{8,12},{9,13},{10,... | collective-permute-start | bytes 393224 | tf_op jit(solution)/shard_map/ppermute | solution.py:114
  83.0 11.5 %collective-permute-start.9 = (bf16[1,256,256]{2,1,0:T(8,128)(2,1)S(1)}, bf16[1,256,256]{2,1,0:T(8,128)(2,1)S(1)}, u32[]{:S(2)}, u32[]{:S(2)}) collective-permute-start(bf16[1,256,256]{2,1,0:T(8,128)(2,1)S(1)} %dynamic-slice_convert_fusion), channel_id=1, source_target_pairs={{0,4},{1,5},{2,6},{3,7},{4,0},{5,1},{6,2},{7,3},{8,12},{9,13},{10,... | collective-permute-start | bytes 393224 | tf_op jit(solution)/shard_map/ppermute | solution.py:114
  91.8 6.9 %copy-start.5 = (bf16[1,256,256]{2,1,0:T(8,128)(2,1)}, bf16[1,256,256]{2,1,0:T(8,128)(2,1)S(1)}, u32[]{:S(2)}) copy-start(bf16[1,256,256]{2,1,0:T(8,128)(2,1)S(1)} %multiply_convert_fusion) | copy-start | bytes 393220
  96.4 2.4 %copy-start.6 = (bf16[256,256]{1,0:T(8,128)(2,1)}, bf16[256,256]{1,0:T(8,128)(2,1)S(1)}, u32[]{:S(2)}) copy-start(bf16[256,256]{1,0:T(8,128)(2,1)S(1)} %fusion.5) | copy-start | bytes 393220
  96.7 2.1 %copy-start.7 = (bf16[256,256]{1,0:T(8,128)(2,1)}, bf16[256,256]{1,0:T(8,128)(2,1)S(1)}, u32[]{:S(2)}) copy-start(bf16[256,256]{1,0:T(8,128)(2,1)S(1)} %fusion.1) | copy-start | bytes 393220
where the time goes:
time: 99.5 us; the launch traced here: 98.7 us
  starting transfers between devices  35.3 us (35%)
  waiting for transfers between devices  16.4 us (16%)
  local copies, waits for them, and re-layouts  10.7 us (11%)
  Pallas kernels  10.5 us (11%)
  blocking collectives  10.4 us (10%)
  other arithmetic  10.1 us (10%)
  matrix products  3.07 us (3%)
  between operations  2.27 us (2%)
    ppermute x6, starting transfers between devices, swap(): return lax.ppermute(array, BOTH, perm)  12.2 us
    pallas_call x4, Pallas kernels, products(): pl.pallas_call(functools.partial(product_kernel, cols, n_fac), out_shape=...  10.5 us
    all_to_all x1, blocking collectives, shards(): part = lax.all_to_all(parts.reshape(nrow, high, tile), 'row', 0, 0)  10.4 us
    ppermute x6, waiting for transfers between devices, swap(): return lax.ppermute(array, BOTH, perm)  9.32 us
    ppermute x2, starting transfers between devices, spread(): lax.ppermute(piece, BOTH, perm)  7 us
    all_to_all x1, starting transfers between devices, shards(): part = lax.all_to_all(part.reshape(ncol, high // ncol, tile), 'col', 0, 0)  5.9 us
    add x4, other arithmetic, shards(): summed = keep.astype(F32) + got.astype(F32)  4.3 us
    ppermute x2, waiting for transfers between devices, spread(): lax.ppermute(piece, BOTH, perm)  3.67 us
  transfers between devices with their start and end apart: 13, of which 6 were waited for; matrix products, arithmetic and copies ran while one was open for 17% of the time, Pallas kernels for 6%

commit v1 on v0

v1 whole, which is shorter than its diff:
```python
import functools

import jax
import jax.numpy as jnp
from jax import lax
from jax.experimental import pallas as pl
from jax.experimental.pallas import tpu as pltpu
from jax.sharding import PartitionSpec as P

F32, BF16 = jnp.float32, jnp.bfloat16
BOTH = ("row", "col")


def transposed_dot(a, b):
    return lax.dot_general(a, b, (((0,), (0,)), ((), ())), preferred_element_type=F32)


def column_kernel(members, keep_one, got_one, keep_two, got_two, link, column_one, column_two):
    member = [members[k].astype(F32) for k in range(2)]
    one = -member[0] * (keep_one[...].astype(F32) + got_one[...].astype(F32))
    column_one[...] = one.astype(BF16)
    two = keep_two[...].astype(F32) + got_two[...].astype(F32)
    two += jnp.dot(column_one[...], link[...], preferred_element_type=F32)
    column_two[...] = (-member[1] * two).astype(BF16)


def diagonal_kernel(sums, link, inverse_one, inverse_two, diag_one, cross, diag_two):
    diag_one[...] = (inverse_one[...] + sums[0].astype(F32)).astype(BF16)
    step = jnp.dot(diag_one[...], link[...], preferred_element_type=F32)
    cross[...] = (sums[1].astype(F32) - step).astype(BF16)
    two = inverse_two[...] + sums[2].astype(F32) - transposed_dot(sums[1], link[...])
    diag_two[...] = (two - transposed_dot(link[...], cross[...])).astype(BF16)


def small_kernel(body, n_out, n_dots, tile, operands, scalars=0):
    memory = [pltpu.SMEM] * scalars + [pltpu.VMEM] * (len(operands) - scalars)
    return pl.pallas_call(
        body,
        out_shape=(jax.ShapeDtypeStruct((tile, tile), BF16),) * n_out,
        in_specs=[pl.BlockSpec(memory_space=space) for space in memory],
        out_specs=[pl.BlockSpec(memory_space=pltpu.VMEM)] * n_out,
        cost_estimate=pl.CostEstimate(
            flops=2 * n_dots * tile**3,
            bytes_accessed=4 * len(operands) * tile**2,
            transcendentals=0,
        ),
    )(*operands)


def product_kernel(cols, n_fac, ids, marks, flags, *refs):
    anc, column = refs[:2]
    factors, (away, keep, sums, acc) = refs[2 : 2 + n_fac], refs[2 + n_fac :]
    step, half = pl.program_id(0), pl.num_programs(0) // 2
    s = ids[step]

    @pl.when(step == 0)
    def _():
        sums[...] = jnp.zeros_like(sums)

    acc[...] = jnp.zeros_like(acc)
    for j in range(cols):

        @pl.when(marks[s * cols + j] > 0)
        def _(j=j):
            acc[...] += jnp.dot(anc[0, j], column[j], preferred_element_type=F32)

    low = acc[...].astype(BF16)

    @pl.when(step < half)
    def _():
        away[0] = low

    @pl.when(step >= half)
    def _():
        keep[0] = low

    for k in range(n_fac):

        @pl.when(flags[s * n_fac + k] > 0)
        def _(k=k):
            pair = (low, factors[k][0]) if k else (factors[k][0], low)
            sums[k] += transposed_dot(*pair)


def products(ids, marks, flags, ancestor, column, factors):
    rows, cols, tile, _ = ancestor.shape
    n, n_fac = ids.shape[0], len(factors)
    block = lambda i, ids, *_: (ids[i], 0, 0)
    return pl.pallas_call(
        functools.partial(product_kernel, cols, n_fac),
        out_shape=(
            jax.ShapeDtypeStruct((n // 2, tile, tile), BF16),
            jax.ShapeDtypeStruct((n // 2, tile, tile), BF16),
            jax.ShapeDtypeStruct((n_fac, tile, tile), F32),
        ),
        grid_spec=pltpu.PrefetchScalarGridSpec(
            num_scalar_prefetch=3,
            grid=(n,),
            in_specs=[
                pl.BlockSpec((1, cols, tile, tile), lambda i, ids, *_: (ids[i], 0, 0, 0)),
                pl.BlockSpec((cols, tile, tile), lambda i, *_: (0, 0, 0)),
            ]
            + [pl.BlockSpec((1, tile, tile), block)] * n_fac,
            out_specs=[
                pl.BlockSpec((1, tile, tile), lambda i, *_: (jnp.minimum(i, n // 2 - 1), 0, 0)),
                pl.BlockSpec((1, tile, tile), lambda i, *_: (jnp.maximum(i - n // 2, 0), 0, 0)),
                pl.BlockSpec((n_fac, tile, tile), lambda i, *_: (0, 0, 0)),
            ],
            scratch_shapes=[pltpu.VMEM((tile, tile), F32)],
        ),
        compiler_params=pltpu.CompilerParams(vmem_limit_bytes=32 << 20),
        cost_estimate=pl.CostEstimate(
            flops=2 * n * (cols + n_fac) * tile**3,
            bytes_accessed=2 * n * (cols + n_fac + 1) * tile**2,
            transcendentals=0,
        ),
    )(ids, marks, flags, ancestor, column, *factors)


def shards(
    ancestor,
    tile_mask,
    member_one,
    member_two,
    factor_one,
    factor_two,
    link_block,
    inverse_one,
    inverse_two,
):
    nrow, ncol = lax.axis_size("row"), lax.axis_size("col")
    row, col = lax.axis_index("row"), lax.axis_index("col")
    rows, cols, tile = ancestor.shape[0], ancestor.shape[1], ancestor.shape[-1]
    group = ncol // nrow
    bits = ncol.bit_length() - 1
    owner = col // group
    at = lambda r, c: r * ncol + c

    def spread(factor):
        have = piece = lax.dynamic_slice_in_dim(factor, col % group * cols, cols, 0)
        for k in range(2, nrow, 2):
            perm = [(at(c // group, c), at((c // group + k) % nrow, c)) for c in range(ncol)]
            have = jnp.where((row - owner) % nrow == k, lax.ppermute(piece, BOTH, perm), have)
        perm = [
            (at(2 * y + c // group % 2, c), at(2 * y + 1 - c // group % 2, c))
            for y in range(nrow // 2)
            for c in range(ncol)
        ]
        return jnp.where((row - owner) % 2 == 0, have, lax.ppermute(have, BOTH, perm))

    def pick(array, bit, other):
        split = array.reshape(array.shape[0] // 2, 2, tile, tile)
        return lax.dynamic_slice_in_dim(split, (col >> bit & 1) ^ other, 1, 1)[:, 0].astype(F32)

    def swap(array, bit):
        perm = [(at(r, c), at(r, c ^ (1 << bit))) for r in range(nrow) for c in range(ncol)]
        return lax.ppermute(array, BOTH, perm)

    def swap_rows(array, bit):
        perm = [(at(r, c), at(r ^ (1 << bit), c)) for r in range(nrow) for c in range(ncol)]
        return lax.ppermute(array, BOTH, perm)

    flags_one = lax.dynamic_slice_in_dim(member_one, row * rows, rows, 0)
    flags_two = lax.dynamic_slice_in_dim(member_two, row * rows, rows, 0)
    marks = [
        (tile_mask * lax.dynamic_slice_in_dim(m, col * cols, cols, 0)[None]).reshape(-1)
        for m in (member_one, member_two)
    ]
    flags = [jnp.stack([flags_one, flags_one * flags_two], 1).reshape(-1), flags_two]
    ids = jnp.arange(rows // 2, dtype=jnp.int32) * 2
    ids = jnp.concatenate([ids + (1 - col % 2), ids + col % 2])

    totals, contracted, arrived = [], [], []
    factors = [(factor_one, factor_two), (factor_two,)]
    for k, factor in enumerate((factor_one, factor_two)):
        column = spread(factor)
        away, keep, part = products(ids, marks[k], flags[k], ancestor, column, factors[k])
        contracted.append(part)
        got = swap(away, 0)
        arrived.append([got])
        for bit in range(1, bits):
            away = (pick(keep, bit, 1) + pick(got, bit, 1)).astype(BF16)
            keep = pick(keep, bit, 0) + pick(got, bit, 0)
            got = swap(away, bit)
            arrived[k].append(got)
        totals += [keep[0], got[0]]

    parts = jnp.concatenate(contracted)
    shape = parts.shape
    part = parts.reshape(-1, tile)
    row_bits = range(nrow.bit_length() - 1)
    for bit in row_bits:
        half = part.shape[0] // 2
        if bit == 1:
            part, _ = lax.optimization_barrier((part, arrived[0][0]))
        mine = row >> bit & 1
        got = swap_rows(lax.dynamic_slice_in_dim(part, (1 - mine) * half, half, 0).astype(BF16), bit)
        part = lax.dynamic_slice_in_dim(part, mine * half, half, 0) + got.astype(F32)
    part = part.astype(BF16)
    after = [None] + [arrived[0][1]] * (bits - 2) + [arrived[1][0]]
    for bit in range(bits):
        if bit:
            part, _ = lax.optimization_barrier((part, after[bit]))
        part = (part.astype(F32) + swap(part, bit).astype(F32)).astype(BF16)
    for bit in reversed(row_bits):
        part, _ = lax.optimization_barrier((part, arrived[1][1] if bit == 0 else arrived[0][-1]))
        got = swap_rows(part, bit)
        low = (row >> bit & 1) == 0
        part = jnp.concatenate([jnp.where(low, part, got), jnp.where(low, got, part)])

    members = jnp.stack([lax.dynamic_index_in_dim(m, col, keepdims=False) for m in (flags_one, flags_two)])
    column_one, column_two = small_kernel(
        column_kernel, 2, 1, tile, (members, *totals, link_block), 1
    )
    diag_one, cross_block, diag_two = small_kernel(
        diagonal_kernel, 3, 3, tile, (part.reshape(shape), link_block, inverse_one, inverse_two)
    )
    return (column_one[None], column_two[None], diag_one, cross_block, diag_two)


def solution(mesh):
    in_specs = (
        P("row", "col", None, None),
        P("row", "col"),
        P(),
        P(),
        P("row", None, None),
        P("row", None, None),
        P(),
        P(),
        P(),
    )
    out_specs = (P(("row", "col"), None, None), P(("row", "col"), None, None), P(), P(), P())
    return jax.shard_map(shards, mesh=mesh, in_specs=in_specs, out_specs=out_specs, check_vma=False)
```

time: 99.5 us -> 98.8 us (level)
  waiting for transfers between devices: 16.4 us -> 42.4 us
  starting transfers between devices: 35.3 us -> 19.6 us
  blocking collectives: 10.4 us -> 0 us
  Pallas kernels: 10.5 us -> 16 us
  matrix products: 3.07 us -> 0 us
  local copies, waits for them, and re-layouts: 10.7 us -> 9.1 us
  between operations: 2.27 us -> 0.97 us
    ppermute x6 -> x9, waiting for transfers between devices: 9.32 us -> 35.4 us  [swap(): return lax.ppermute(array, BOTH, perm)]
    all_to_all x3 -> x0, starting transfers between devices: 12.7 us -> none  [the longest x1 5.9 us: shards(): part = lax.all_to_all(part.reshape(ncol, high // ncol, tile), 'col', 0, 0)]
    all_to_all x1 -> x0, blocking collectives: 10.4 us -> none  [shards(): part = lax.all_to_all(parts.reshape(nrow, high, tile), 'row', 0, 0)]
    ppermute x6 -> x9, starting transfers between devices: 12.2 us -> 6.09 us  [swap(): return lax.ppermute(array, BOTH, perm)]
    ppermute x0 -> x4, waiting for transfers between devices: none -> 4.5 us  [swap_rows(): return lax.ppermute(array, BOTH, perm)]
    pallas_call x0 -> x2, Pallas kernels: none -> 4.33 us  [small_kernel(): pl.pallas_call(body, out_shape=(jax.ShapeDtypeStruct((tile, tile), BF16),...]
    ppermute x0 -> x4, starting transfers between devices: none -> 3.91 us  [swap_rows(): return lax.ppermute(array, BOTH, perm)]
    all_to_all x3 -> x0, waiting for transfers between devices: 3.43 us -> none  [the longest x1 2.74 us: shards(): part = lax.all_to_all(part.reshape(ncol, high // ncol, tile), 'col', 0, 0)]
  transfers between devices with their start and end apart: 13 -> 17, of which waited for: 6 -> 10; matrix products, arithmetic and copies ran while one was open for 17% -> 14% of each run, Pallas kernels for 6% -> 14%
where the time goes in v1:
time: 98.8 us; the launch traced here: 97.6 us
  waiting for transfers between devices  42.4 us (43%)
  starting transfers between devices  19.6 us (20%)
  Pallas kernels  16 us (16%)
  other arithmetic  9.41 us (10%)
  local copies, waits for them, and re-layouts  9.1 us (9%)
    ppermute x9, waiting for transfers between devices, swap(): return lax.ppermute(array, BOTH, perm)  35.4 us
    pallas_call x2, Pallas kernels, products(): pl.pallas_call(functools.partial(product_kernel, cols, n_fac), out_shape=...  11.7 us
    ppermute x2, starting transfers between devices, spread(): lax.ppermute(piece, BOTH, perm)  7 us
    ppermute x9, starting transfers between devices, swap(): return lax.ppermute(array, BOTH, perm)  6.09 us
    ppermute x4, waiting for transfers between devices, swap_rows(): return lax.ppermute(array, BOTH, perm)  4.5 us
    pallas_call x2, Pallas kernels, small_kernel(): pl.pallas_call(body, out_shape=(jax.ShapeDtypeStruct((tile, tile), BF16),...  4.33 us
    ppermute x4, starting transfers between devices, swap_rows(): return lax.ppermute(array, BOTH, perm)  3.91 us
    dynamic_slice x2, local copies, waits for them, and re-layouts, spread(): have = piece = lax.dynamic_slice_in_dim(factor, col % group * cols, cols, 0)  3.09 us
  transfers between devices with their start and end apart: 17, of which 10 were waited for; matrix products, arithmetic and copies ran while one was open for 14% of the time, Pallas kernels for 14%

profile of v1, /device:TPU:0, one launch (start us, length us, event | category | flops | bytes accessed | tf_op | source)
XLA Modules:
  0.0 97.6 jit_solution(852596647546914131)
XLA Ops:
  0.7 1.2 %constant_dynamic-slice_fusion.1 = bf16[4,256,256]{2,1,0:T(8,128)(2,1)S(1)} fusion(bf16[8,256,256]{2,1,0:T(8,128)(2,1)} %refs_2_.2, s32[]{:T(128)S(6)} %select_n.143), kind=kLoop, calls=%fused_computation.33 | loop fusion | bytes 1048580 | tf_op jit(solution)/shard_map/dynamic_slice | solution.py:140
  1.9 4.9 %collective-permute-start = (bf16[4,256,256]{2,1,0:T(8,128)(2,1)S(1)}, bf16[4,256,256]{2,1,0:T(8,128)(2,1)S(1)}, u32[]{:S(2)}, u32[]{:S(2)}) collective-permute-start(bf16[4,256,256]{2,1,0:T(8,128)(2,1)S(1)} %constant_dynamic-slice_fusion.1), channel_id=1, source_target_pairs={{0,16},{1,17},{10,26},{11,27},{20,4},{21,5},{30,14},{31,15}} | collective-permute-start | bytes 1572872 | tf_op jit(solution)/shard_map/ppermute | solution.py:143
  6.8 1.9 %constant_dynamic-slice_fusion = bf16[4,256,256]{2,1,0:T(8,128)(2,1)} fusion(bf16[8,256,256]{2,1,0:T(8,128)(2,1)} %refs_2_.3, s32[]{:T(128)S(6)} %select_n.143), kind=kLoop, calls=%fused_computation.32 | loop fusion | bytes 1048580 | tf_op jit(solution)/shard_map/dynamic_slice | solution.py:140
  8.7 2.1 %collective-permute-start.5 = (bf16[4,256,256]{2,1,0:T(8,128)(2,1)}, bf16[4,256,256]{2,1,0:T(8,128)(2,1)}, u32[]{:S(2)}, u32[]{:S(2)}) collective-permute-start(bf16[4,256,256]{2,1,0:T(8,128)(2,1)} %constant_dynamic-slice_fusion), channel_id=1, source_target_pairs={{0,16},{1,17},{10,26},{11,27},{20,4},{21,5},{30,14},{31,15}} | collective-permute-start | bytes 1572872 | tf_op jit(solution)/shard_map/ppermute | solution.py:143
  13.7 1.1 %broadcast_select_fusion.1 = bf16[4,256,256]{2,1,0:T(8,128)(2,1)S(1)} fusion(bf16[4,256,256]{2,1,0:T(8,128)(2,1)S(1)} %collective-permute-done, pred[]{:T(512)S(6)} %eq.24, bf16[8,256,256]{2,1,0:T(8,128)(2,1)} %refs_2_.2, s32[]{:T(128)S(6)} %select_n.143), kind=kLoop, calls=%fused_computation.6 | loop fusion | flops 262144 | bytes 1572869 | tf_op jit(solution)/shard_map/jit(_where)/select_n | solution.py:143
  14.8 1.3 %collective-permute-start.1 = (bf16[4,256,256]{2,1,0:T(8,128)(2,1)S(1)}, bf16[4,256,256]{2,1,0:T(8,128)(2,1)S(1)}, u32[]{:S(2)}, u32[]{:S(2)}) collective-permute-start(bf16[4,256,256]{2,1,0:T(8,128)(2,1)S(1)} %broadcast_select_fusion.1), channel_id=1, source_target_pairs={{0,8},{1,9},{10,2},{11,3},{4,12},{5,13},{14,6},{15,7},{16,24},{17,... | collective-permute-start | bytes 1572872 | tf_op jit(solution)/shard_map/ppermute | solution.py:149
  16.7 2.5 %collective-permute-done.5 = bf16[4,256,256]{2,1,0:T(8,128)(2,1)} collective-permute-done((bf16[4,256,256]{2,1,0:T(8,128)(2,1)}, bf16[4,256,256]{2,1,0:T(8,128)(2,1)}, u32[]{:S(2)}, u32[]{:S(2)}) %collective-permute-start.5) | collective-permute-done | bytes 524320 | tf_op jit(solution)/shard_map/ppermute | solution.py:143
  19.2 1.3 %collective-permute-start.6 = (bf16[4,256,256]{2,1,0:T(8,128)(2,1)S(1)}, bf16[4,256,256]{2,1,0:T(8,128)(2,1)S(1)}, u32[]{:S(2)}, u32[]{:S(2)}) collective-permute-start(bf16[4,256,256]{2,1,0:T(8,128)(2,1)S(1)} %broadcast_select_fusion), channel_id=1, source_target_pairs={{0,8},{1,9},{10,2},{11,3},{4,12},{5,13},{14,6},{15,7},{16,24},{17,... | collective-permute-start | bytes 1572872 | tf_op jit(solution)/shard_map/ppermute | solution.py:149
  20.7 2.2 %copy-done = bf16[8,4,256,256]{3,2,1,0:T(8,128)(2,1)S(1)} copy-done((bf16[8,4,256,256]{3,2,1,0:T(8,128)(2,1)S(1)}, bf16[8,4,256,256]{3,2,1,0:T(8,128)(2,1)}, u32[]{:S(2)}) %copy-start) | copy-done | bytes 4194328
  22.9 6.9 %shard_map.128 = (bf16[4,256,256]{2,1,0:T(8,128)(2,1)}, bf16[4,256,256]{2,1,0:T(8,128)(2,1)S(1)}, f32[2,256,256]{2,1,0:T(8,128)S(1)}) custom-call(s32[8]{0:T(128)S(1)} %pad_add_fusion.2.ids, s32[32]{0:T(128)S(1)} %reshape.111.marks, s32[16]{0:T(128)S(1)} %reshape.112.flags, bf16[8,4,256,256]{3,2,1,0:T(8,128)(2,1)S(1)} %copy-done, ...), custom_call_target="tpu_custom_call" | custom-call | flops 1610612736 | bytes 7340032 | tf_op jit(solution)/shard_map/pallas_call | solution.py:89
  29.9 4.8 %shard_map.129 = (bf16[4,256,256]{2,1,0:T(8,128)(2,1)S(1)}, bf16[4,256,256]{2,1,0:T(8,128)(2,1)S(1)}, f32[1,256,256]{2,1,0:T(8,128)S(1)}) custom-call(s32[8]{0:T(128)S(1)} %pad_add_fusion.2.ids, s32[32]{0:T(128)S(1)} %reshape.117.marks, s32[8]{0:T(128)S(1)} %get-tuple-element.38.flags, bf16[8,4,256,256]{3,2,1,0:T(8,128)(2,1)S(1)} %copy-done.1, ...), custom_call_target="tpu_custom_call" | custom-call | flops 1342177280 | bytes 6291456 | tf_op jit(solution)/shard_map/pallas_call | solution.py:89
  34.9 1.4 %collective-permute-start.7 = (bf16[4,256,256]{2,1,0:T(8,128)(2,1)S(1)}, bf16[4,256,256]{2,1,0:T(8,128)(2,1)S(1)}, u32[]{:S(2)}, u32[]{:S(2)}) collective-permute-start(bf16[4,256,256]{2,1,0:T(8,128)(2,1)S(1)} %get-tuple-element.24), channel_id=1, source_target_pairs={{0,1},{1,0},{2,3},{3,2},{4,5},{5,4},{6,7},{7,6},{8,9},{9,8},{10,11... | collective-permute-start | bytes 1572872 | tf_op jit(solution)/shard_map/ppermute | solution.py:157
  36.4 7.8 %collective-permute-done.2 = bf16[4,256,256]{2,1,0:T(8,128)(2,1)} collective-permute-done((bf16[4,256,256]{2,1,0:T(8,128)(2,1)}, bf16[4,256,256]{2,1,0:T(8,128)(2,1)}, u32[]{:S(2)}, u32[]{:S(2)}) %collective-permute-start.2) | collective-permute-done | bytes 524320 | tf_op jit(solution)/shard_map/ppermute | solution.py:157
  44.2 2.2 %collective-permute-start.11 = (bf16[192,256]{1,0:T(8,128)(2,1)S(1)}, bf16[192,256]{1,0:T(8,128)(2,1)S(1)}, u32[]{:S(2)}, u32[]{:S(2)}) collective-permute-start(bf16[192,256]{1,0:T(8,128)(2,1)S(1)} %dynamic-slice_convert_fusion.1), channel_id=1, source_target_pairs={{0,16},{1,17},{2,18},{3,19},{4,20},{5,21},{6,22},{7,23},{8,24},{9,... | collective-permute-start | bytes 294920 | tf_op jit(solution)/shard_map/ppermute | solution.py:161
  46.4 1.0 %fusion = bf16[2,256,256]{2,1,0:T(8,128)(2,1)S(1)} fusion(bf16[2,2,256,256]{3,2,1,0:T(8,128)(2,1)} %bitcast.3, s32[]{:T(128)S(6)} %select_n.148, bf16[2,2,256,256]{3,2,1,0:T(8,128)(2,1)S(1)} %bitcast.48), kind=kLoop, calls=%fused_computation.12 | loop fusion | flops 524288 | bytes 786436 | tf_op jit(solution)/shard_map/convert_element_type | solution.py:182
  47.4 1.5 %collective-permute-done.11 = bf16[192,256]{1,0:T(8,128)(2,1)S(1)} collective-permute-done((bf16[192,256]{1,0:T(8,128)(2,1)S(1)}, bf16[192,256]{1,0:T(8,128)(2,1)S(1)}, u32[]{:S(2)}, u32[]{:S(2)}) %collective-permute-start.11) | collective-permute-done | bytes 98336 | tf_op jit(solution)/shard_map/ppermute | solution.py:161
  49.1 4.3 %collective-permute-done.7 = bf16[4,256,256]{2,1,0:T(8,128)(2,1)S(1)} collective-permute-done((bf16[4,256,256]{2,1,0:T(8,128)(2,1)S(1)}, bf16[4,256,256]{2,1,0:T(8,128)(2,1)S(1)}, u32[]{:S(2)}, u32[]{:S(2)}) %collective-permute-start.7) | collective-permute-done | bytes 524320 | tf_op jit(solution)/shard_map/ppermute | solution.py:157
  53.5 0.9 collective-permute-done.12
  54.5 1.2 %collective-permute-start.13 = (bf16[192,256]{1,0:T(8,128)(2,1)S(1)}, bf16[192,256]{1,0:T(8,128)(2,1)S(1)}, u32[]{:S(2)}, u32[]{:S(2)}) collective-permute-start(bf16[192,256]{1,0:T(8,128)(2,1)S(1)} %add_convert_fusion.4), channel_id=1, source_target_pairs={{0,2},{1,3},{2,0},{3,1},{4,6},{5,7},{6,4},{7,5},{8,10},{9,11},{10,... | collective-permute-start | bytes 294920 | tf_op jit(solution)/shard_map/ppermute | solution.py:157
  55.6 1.0 %convert_add_fusion.1 = f32[2,1,256,256]{3,2,1,0:T(8,128)S(1)} fusion(bf16[2,2,256,256]{3,2,1,0:T(8,128)(2,1)} %bitcast.3, s32[]{:T(128)S(6)} %select_n.146, bf16[2,2,256,256]{3,2,1,0:T(8,128)(2,1)S(1)} %bitcast.49), kind=kLoop, calls=%fused_computation.4 | loop fusion | flops 393216 | bytes 1048580 | tf_op jit(solution)/shard_map/add | solution.py:183
  56.6 6.8 %collective-permute-done.13 = bf16[192,256]{1,0:T(8,128)(2,1)S(1)} collective-permute-done((bf16[192,256]{1,0:T(8,128)(2,1)S(1)}, bf16[192,256]{1,0:T(8,128)(2,1)S(1)}, u32[]{:S(2)}, u32[]{:S(2)}) %collective-permute-start.13) | collective-permute-done | bytes 98336 | tf_op jit(solution)/shard_map/ppermute | solution.py:157
  63.5 3.3 %collective-permute-start.14 = (bf16[192,256]{1,0:T(8,128)(2,1)S(1)}, bf16[192,256]{1,0:T(8,128)(2,1)S(1)}, u32[]{:S(2)}, u32[]{:S(2)}) collective-permute-start(bf16[192,256]{1,0:T(8,128)(2,1)S(1)} %add_convert_fusion.3), channel_id=1, source_target_pairs={{0,4},{1,5},{2,6},{3,7},{4,0},{5,1},{6,2},{7,3},{8,12},{9,13},{10,... | collective-permute-start | bytes 294920 | tf_op jit(solution)/shard_map/ppermute | solution.py:157
  67.6 7.2 %collective-permute-done.14 = bf16[192,256]{1,0:T(8,128)(2,1)S(1)} collective-permute-done((bf16[192,256]{1,0:T(8,128)(2,1)S(1)}, bf16[192,256]{1,0:T(8,128)(2,1)S(1)}, u32[]{:S(2)}, u32[]{:S(2)}) %collective-permute-start.14) | collective-permute-done | bytes 98336 | tf_op jit(solution)/shard_map/ppermute | solution.py:157
  74.8 1.8 %collective-permute-done.4 = bf16[1,256,256]{2,1,0:T(8,128)(2,1)S(1)} collective-permute-done((bf16[1,256,256]{2,1,0:T(8,128)(2,1)S(1)}, bf16[1,256,256]{2,1,0:T(8,128)(2,1)S(1)}, u32[]{:S(2)}, u32[]{:S(2)}) %collective-permute-start.4) | collective-permute-done | bytes 131104 | tf_op jit(solution)/shard_map/ppermute | solution.py:157
  76.6 1.6 %collective-permute-start.15 = (bf16[192,256]{1,0:T(8,128)(2,1)S(1)}, bf16[192,256]{1,0:T(8,128)(2,1)S(1)}, u32[]{:S(2)}, u32[]{:S(2)}) collective-permute-start(bf16[192,256]{1,0:T(8,128)(2,1)S(1)} %add_convert_fusion.2), channel_id=1, source_target_pairs={{0,16},{1,17},{2,18},{3,19},{4,20},{5,21},{6,22},{7,23},{8,24},{9,... | collective-permute-start | bytes 294920 | tf_op jit(solution)/shard_map/ppermute | solution.py:161
  78.3 3.0 %collective-permute-done.15 = bf16[192,256]{1,0:T(8,128)(2,1)S(1)} collective-permute-done((bf16[192,256]{1,0:T(8,128)(2,1)S(1)}, bf16[192,256]{1,0:T(8,128)(2,1)S(1)}, u32[]{:S(2)}, u32[]{:S(2)}) %collective-permute-start.15) | collective-permute-done | bytes 98336 | tf_op jit(solution)/shard_map/ppermute | solution.py:161
  81.4 0.8 fusion.2
  83.3 1.8 %pad_add_fusion.1.members = s32[2]{0:T(128)} fusion(s32[1]{0:T(128)} %dynamic_slice.73, s32[1]{0:T(128)} %dynamic_slice.72), kind=kLoop, calls=%fused_computation.37 | loop fusion | flops 2 | bytes 16 | tf_op jit(solution)/shard_map/stack | solution.py:211
  85.2 6.6 %collective-permute-done.9 = bf16[1,256,256]{2,1,0:T(8,128)(2,1)S(1)} collective-permute-done((bf16[1,256,256]{2,1,0:T(8,128)(2,1)S(1)}, bf16[1,256,256]{2,1,0:T(8,128)(2,1)S(1)}, u32[]{:S(2)}, u32[]{:S(2)}) %collective-permute-start.9) | collective-permute-done | bytes 131104 | tf_op jit(solution)/shard_map/ppermute | solution.py:157
  92.4 2.1 %shard_map.130 = (bf16[256,256]{1,0:T(8,128)(2,1)}, bf16[256,256]{1,0:T(8,128)(2,1)}) custom-call(s32[2]{0:T(128)} %pad_add_fusion.1.members, f32[256,256]{1,0:T(8,128)} %get-tuple-element.42.keep_one, bf16[256,256]{1,0:T(8,128)(2,1)} %bitcast.55, f32[256,256]{1,0:T(8,128)} %get-tuple-element.40.keep_two, bf16[256,256]{1,0:T(8,128)(2,1)} %bitcast.56, ...), custom_call_target="tpu_custom_call" | custom-call | flops 33554432 | bytes 1572864 | tf_op jit(solution)/shard_map/pallas_call | solution.py:37
  94.5 0.8 pad_maximum_fusion.1
  95.3 2.3 %shard_map.131 = (bf16[256,256]{1,0:T(8,128)(2,1)}, bf16[256,256]{1,0:T(8,128)(2,1)}, bf16[256,256]{1,0:T(8,128)(2,1)}) custom-call(bf16[3,256,256]{2,1,0:T(8,128)(2,1)} %bitcast.52, bf16[256,256]{1,0:T(8,128)(2,1)} %link.3, f32[256,256]{1,0:T(8,128)} %inverse_one.1, f32[256,256]{1,0:T(8,128)} %inverse_two.1), custom_call_target="tpu_custom_call" | custom-call | flops 100663296 | bytes 1048576 | tf_op jit(solution)/shard_map/pallas_call | solution.py:37
  (62 shorter events, 7.2 us)
Async XLA Ops:
  0.6 20.1 %copy-start.3 = (bf16[8,256,256]{2,1,0:T(8,128)(2,1)S(1)}, bf16[8,256,256]{2,1,0:T(8,128)(2,1)}, u32[]{:S(2)}) copy-start(bf16[8,256,256]{2,1,0:T(8,128)(2,1)} %refs_2_.2) | copy-start | bytes 3145732
  0.6 18.5 %copy-start.2 = (bf16[8,256,256]{2,1,0:T(8,128)(2,1)S(1)}, bf16[8,256,256]{2,1,0:T(8,128)(2,1)}, u32[]{:S(2)}) copy-start(bf16[8,256,256]{2,1,0:T(8,128)(2,1)} %refs_2_.3) | copy-start | bytes 3145732
  1.9 11.8 %collective-permute-start = (bf16[4,256,256]{2,1,0:T(8,128)(2,1)S(1)}, bf16[4,256,256]{2,1,0:T(8,128)(2,1)S(1)}, u32[]{:S(2)}, u32[]{:S(2)}) collective-permute-start(bf16[4,256,256]{2,1,0:T(8,128)(2,1)S(1)} %constant_dynamic-slice_fusion.1), channel_id=1, source_target_pairs={{0,16},{1,17},{10,26},{11,27},{20,4},{21,5},{30,14},{31,15}} | collective-permute-start | bytes 1572872 | tf_op jit(solution)/shard_map/ppermute | solution.py:143
  8.7 10.5 %collective-permute-start.5 = (bf16[4,256,256]{2,1,0:T(8,128)(2,1)}, bf16[4,256,256]{2,1,0:T(8,128)(2,1)}, u32[]{:S(2)}, u32[]{:S(2)}) collective-permute-start(bf16[4,256,256]{2,1,0:T(8,128)(2,1)} %constant_dynamic-slice_fusion), channel_id=1, source_target_pairs={{0,16},{1,17},{10,26},{11,27},{20,4},{21,5},{30,14},{31,15}} | collective-permute-start | bytes 1572872 | tf_op jit(solution)/shard_map/ppermute | solution.py:143
  14.8 5.8 %collective-permute-start.1 = (bf16[4,256,256]{2,1,0:T(8,128)(2,1)S(1)}, bf16[4,256,256]{2,1,0:T(8,128)(2,1)S(1)}, u32[]{:S(2)}, u32[]{:S(2)}) collective-permute-start(bf16[4,256,256]{2,1,0:T(8,128)(2,1)S(1)} %broadcast_select_fusion.1), channel_id=1, source_target_pairs={{0,8},{1,9},{10,2},{11,3},{4,12},{5,13},{14,6},{15,7},{16,24},{17,... | collective-permute-start | bytes 1572872 | tf_op jit(solution)/shard_map/ppermute | solution.py:149
  19.2 10.6 %collective-permute-start.6 = (bf16[4,256,256]{2,1,0:T(8,128)(2,1)S(1)}, bf16[4,256,256]{2,1,0:T(8,128)(2,1)S(1)}, u32[]{:S(2)}, u32[]{:S(2)}) collective-permute-start(bf16[4,256,256]{2,1,0:T(8,128)(2,1)S(1)} %broadcast_select_fusion), channel_id=1, source_target_pairs={{0,8},{1,9},{10,2},{11,3},{4,12},{5,13},{14,6},{15,7},{16,24},{17,... | collective-permute-start | bytes 1572872 | tf_op jit(solution)/shard_map/ppermute | solution.py:149
  20.7 2.2 %copy-start = (bf16[8,4,256,256]{3,2,1,0:T(8,128)(2,1)S(1)}, bf16[8,4,256,256]{3,2,1,0:T(8,128)(2,1)}, u32[]{:S(2)}) copy-start(bf16[8,4,256,256]{3,2,1,0:T(8,128)(2,1)} %refs_0_.3) | copy-start | bytes 12582916
  22.9 7.0 %copy-start.1 = (bf16[8,4,256,256]{3,2,1,0:T(8,128)(2,1)S(1)}, bf16[8,4,256,256]{3,2,1,0:T(8,128)(2,1)}, u32[]{:S(2)}) copy-start(bf16[8,4,256,256]{3,2,1,0:T(8,128)(2,1)} %refs_0_.3) | copy-start | bytes 12582916
  29.8 14.3 %collective-permute-start.2 = (bf16[4,256,256]{2,1,0:T(8,128)(2,1)}, bf16[4,256,256]{2,1,0:T(8,128)(2,1)}, u32[]{:S(2)}, u32[]{:S(2)}) collective-permute-start(bf16[4,256,256]{2,1,0:T(8,128)(2,1)} %get-tuple-element.22), channel_id=1, source_target_pairs={{0,1},{1,0},{2,3},{3,2},{4,5},{5,4},{6,7},{7,6},{8,9},{9,8},{10,11... | collective-permute-start | bytes 1572872 | tf_op jit(solution)/shard_map/ppermute | solution.py:157
  34.8 1.5 %collective-permute-start.10 = (bf16[384,256]{1,0:T(8,128)(2,1)S(1)}, bf16[384,256]{1,0:T(8,128)(2,1)S(1)}, u32[]{:S(2)}, u32[]{:S(2)}) collective-permute-start(bf16[384,256]{1,0:T(8,128)(2,1)S(1)} %dynamic-slice_convert_fusion), channel_id=1, source_target_pairs={{0,8},{1,9},{2,10},{3,11},{4,12},{5,13},{6,14},{7,15},{8,0},{9,1},... | collective-permute-start | bytes 589832 | tf_op jit(solution)/shard_map/ppermute | solution.py:161
  34.9 18.4 %collective-permute-start.7 = (bf16[4,256,256]{2,1,0:T(8,128)(2,1)S(1)}, bf16[4,256,256]{2,1,0:T(8,128)(2,1)S(1)}, u32[]{:S(2)}, u32[]{:S(2)}) collective-permute-start(bf16[4,256,256]{2,1,0:T(8,128)(2,1)S(1)} %get-tuple-element.24), channel_id=1, source_target_pairs={{0,1},{1,0},{2,3},{3,2},{4,5},{5,4},{6,7},{7,6},{8,9},{9,8},{10,11... | collective-permute-start | bytes 1572872 | tf_op jit(solution)/shard_map/ppermute | solution.py:157
  36.4 45.8 %copy-start.6 = (s32[32]{0:T(128)S(1)}, s32[32]{0:T(128)}, u32[]{:S(2)}) copy-start(s32[32]{0:T(128)} %param.11) | copy-start | bytes 388
  36.4 46.4 %copy-start.7 = (s32[32]{0:T(128)S(1)}, s32[32]{0:T(128)}, u32[]{:S(2)}) copy-start(s32[32]{0:T(128)} %param.12) | copy-start | bytes 388
  44.2 4.8 %collective-permute-start.11 = (bf16[192,256]{1,0:T(8,128)(2,1)S(1)}, bf16[192,256]{1,0:T(8,128)(2,1)S(1)}, u32[]{:S(2)}, u32[]{:S(2)}) collective-permute-start(bf16[192,256]{1,0:T(8,128)(2,1)S(1)} %dynamic-slice_convert_fusion.1), channel_id=1, source_target_pairs={{0,16},{1,17},{2,18},{3,19},{4,20},{5,21},{6,22},{7,23},{8,24},{9,... | collective-permute-start | bytes 294920 | tf_op jit(solution)/shard_map/ppermute | solution.py:161
  47.4 7.1 %collective-permute-start.3 = (bf16[2,256,256]{2,1,0:T(8,128)(2,1)S(1)}, bf16[2,256,256]{2,1,0:T(8,128)(2,1)S(1)}, u32[]{:S(2)}, u32[]{:S(2)}) collective-permute-start(bf16[2,256,256]{2,1,0:T(8,128)(2,1)S(1)} %fusion), channel_id=1, source_target_pairs={{0,2},{1,3},{2,0},{3,1},{4,6},{5,7},{6,4},{7,5},{8,10},{9,11},{10,... | collective-permute-start | bytes 786440 | tf_op jit(solution)/shard_map/ppermute | solution.py:157
  49.0 5.4 %collective-permute-start.12 = (bf16[192,256]{1,0:T(8,128)(2,1)S(1)}, bf16[192,256]{1,0:T(8,128)(2,1)S(1)}, u32[]{:S(2)}, u32[]{:S(2)}) collective-permute-start(bf16[192,256]{1,0:T(8,128)(2,1)S(1)} %add_convert_fusion.5), channel_id=1, source_target_pairs={{0,1},{1,0},{2,3},{3,2},{4,5},{5,4},{6,7},{7,6},{8,9},{9,8},{10,11... | collective-permute-start | bytes 294920 | tf_op jit(solution)/shard_map/ppermute | solution.py:157
  53.4 27.9 %collective-permute-start.8 = (bf16[2,256,256]{2,1,0:T(8,128)(2,1)S(1)}, bf16[2,256,256]{2,1,0:T(8,128)(2,1)S(1)}, u32[]{:S(2)}, u32[]{:S(2)}) collective-permute-start(bf16[2,256,256]{2,1,0:T(8,128)(2,1)S(1)} %fusion.1), channel_id=1, source_target_pairs={{0,2},{1,3},{2,0},{3,1},{4,6},{5,7},{6,4},{7,5},{8,10},{9,11},{10,... | collective-permute-start | bytes 786440 | tf_op jit(solution)/shard_map/ppermute | solution.py:157
  54.5 9.0 %collective-permute-start.13 = (bf16[192,256]{1,0:T(8,128)(2,1)S(1)}, bf16[192,256]{1,0:T(8,128)(2,1)S(1)}, u32[]{:S(2)}, u32[]{:S(2)}) collective-permute-start(bf16[192,256]{1,0:T(8,128)(2,1)S(1)} %add_convert_fusion.4), channel_id=1, source_target_pairs={{0,2},{1,3},{2,0},{3,1},{4,6},{5,7},{6,4},{7,5},{8,10},{9,11},{10,... | collective-permute-start | bytes 294920 | tf_op jit(solution)/shard_map/ppermute | solution.py:157
  63.5 11.3 %collective-permute-start.14 = (bf16[192,256]{1,0:T(8,128)(2,1)S(1)}, bf16[192,256]{1,0:T(8,128)(2,1)S(1)}, u32[]{:S(2)}, u32[]{:S(2)}) collective-permute-start(bf16[192,256]{1,0:T(8,128)(2,1)S(1)} %add_convert_fusion.3), channel_id=1, source_target_pairs={{0,4},{1,5},{2,6},{3,7},{4,0},{5,1},{6,2},{7,3},{8,12},{9,13},{10,... | collective-permute-start | bytes 294920 | tf_op jit(solution)/shard_map/ppermute | solution.py:157
  67.5 9.1 %collective-permute-start.4 = (bf16[1,256,256]{2,1,0:T(8,128)(2,1)S(1)}, bf16[1,256,256]{2,1,0:T(8,128)(2,1)S(1)}, u32[]{:S(2)}, u32[]{:S(2)}) collective-permute-start(bf16[1,256,256]{2,1,0:T(8,128)(2,1)S(1)} %get-tuple-element.41), channel_id=1, source_target_pairs={{0,4},{1,5},{2,6},{3,7},{4,0},{5,1},{6,2},{7,3},{8,12},{9,13},{10,... | collective-permute-start | bytes 393224 | tf_op jit(solution)/shard_map/ppermute | solution.py:157
  76.6 15.1 %copy-start.4 = (bf16[1,256,256]{2,1,0:T(8,128)(2,1)}, bf16[1,256,256]{2,1,0:T(8,128)(2,1)S(1)}, u32[]{:S(2)}) copy-start(bf16[1,256,256]{2,1,0:T(8,128)(2,1)S(1)} %collective-permute-done.4) | copy-start | bytes 393220
  76.6 4.6 %collective-permute-start.15 = (bf16[192,256]{1,0:T(8,128)(2,1)S(1)}, bf16[192,256]{1,0:T(8,128)(2,1)S(1)}, u32[]{:S(2)}, u32[]{:S(2)}) collective-permute-start(bf16[192,256]{1,0:T(8,128)(2,1)S(1)} %add_convert_fusion.2), channel_id=1, source_target_pairs={{0,16},{1,17},{2,18},{3,19},{4,20},{5,21},{6,22},{7,23},{8,24},{9,... | collective-permute-start | bytes 294920 | tf_op jit(solution)/shard_map/ppermute | solution.py:161
  81.3 13.2 %collective-permute-start.16 = (bf16[384,256]{1,0:T(8,128)(2,1)S(1)}, bf16[384,256]{1,0:T(8,128)(2,1)S(1)}, u32[]{:S(2)}, u32[]{:S(2)}) collective-permute-start(bf16[384,256]{1,0:T(8,128)(2,1)S(1)} %pad_maximum_fusion.2), channel_id=1, source_target_pairs={{0,8},{1,9},{2,10},{3,11},{4,12},{5,13},{6,14},{7,15},{8,0},{9,1},... | collective-permute-start | bytes 589832 | tf_op jit(solution)/shard_map/ppermute | solution.py:161
  82.2 9.6 %collective-permute-start.9 = (bf16[1,256,256]{2,1,0:T(8,128)(2,1)S(1)}, bf16[1,256,256]{2,1,0:T(8,128)(2,1)S(1)}, u32[]{:S(2)}, u32[]{:S(2)}) collective-permute-start(bf16[1,256,256]{2,1,0:T(8,128)(2,1)S(1)} %get-tuple-element.39), channel_id=1, source_target_pairs={{0,4},{1,5},{2,6},{3,7},{4,0},{5,1},{6,2},{7,3},{8,12},{9,13},{10,... | collective-permute-start | bytes 393224 | tf_op jit(solution)/shard_map/ppermute | solution.py:157
  91.8 0.7 copy-start.5

commit v2 on v1

v2 whole, which is shorter than its diff:
```python
import functools

import jax
import jax.numpy as jnp
from jax import lax
from jax.experimental import pallas as pl
from jax.experimental.pallas import tpu as pltpu
from jax.sharding import PartitionSpec as P

F32, BF16 = jnp.float32, jnp.bfloat16
BOTH = ("row", "col")


def transposed_dot(a, b):
    return lax.dot_general(a, b, (((0,), (0,)), ((), ())), preferred_element_type=F32)


def wide(ref, k):
    return jnp.concatenate([ref[2 * k], ref[2 * k + 1]], axis=-1)


def column_kernel(first, second, place, link, *refs):
    (keep_one, got_one), halves, (column_one, column_two) = refs[:2], refs[2:-2], refs[-2:]
    member_one, member_two = (m[place[0]].astype(F32) for m in (first, second))
    one = keep_one[...].astype(F32) + got_one[...].astype(F32)
    column_one[...] = (-member_one * one).astype(BF16)
    two = [halves[2 * k][...].astype(F32) + halves[2 * k + 1][...].astype(F32) for k in range(2)]
    two = jnp.concatenate(two, axis=-1)
    two += jnp.dot(column_one[...], link[...], preferred_element_type=F32)
    column_two[...] = (-member_two * two).astype(BF16)


def diagonal_kernel(sums, link, inverse_one, inverse_two, diag_one, cross, diag_two):
    diag_one[...] = (inverse_one[...] + wide(sums, 0).astype(F32)).astype(BF16)
    step = jnp.dot(diag_one[...], link[...], preferred_element_type=F32)
    crossed = wide(sums, 1)
    cross[...] = (crossed.astype(F32) - step).astype(BF16)
    two = inverse_two[...] + wide(sums, 2).astype(F32) - transposed_dot(crossed, link[...])
    diag_two[...] = (two - transposed_dot(link[...], cross[...])).astype(BF16)


def small_kernel(body, n_out, n_dots, tile, operands, scalars=0):
    memory = [pltpu.SMEM] * scalars + [pltpu.VMEM] * (len(operands) - scalars)
    return pl.pallas_call(
        body,
        out_shape=(jax.ShapeDtypeStruct((tile, tile), BF16),) * n_out,
        in_specs=[pl.BlockSpec(memory_space=space) for space in memory],
        out_specs=[pl.BlockSpec(memory_space=pltpu.VMEM)] * n_out,
        cost_estimate=pl.CostEstimate(
            flops=2 * n_dots * tile**3,
            bytes_accessed=4 * len(operands) * tile**2,
            transcendentals=0,
        ),
    )(*operands)


def product_kernel(n_fac, pieces, ids, marks, flags, anc, column, *refs):
    factors, outs = refs[:n_fac], refs[n_fac:-3]
    sums, tiles, sems = refs[-3:]
    n, cols, tile, _ = tiles.shape
    half, width = n // 2, tile // pieces
    fetch = lambda i: pltpu.make_async_copy(anc.at[ids[i]], tiles.at[i], sems.at[i])
    for i in range(n):
        fetch(i).start()
    sums[...] = jnp.zeros_like(sums)
    zero = jnp.zeros((tile, tile), BF16)
    weights = column[...].reshape(cols * tile, tile)

    def step(i, _, outs):
        s = ids[i]
        fetch(i).wait()
        kept = [jnp.where(marks[s * cols + j] > 0, tiles[i, j], zero) for j in range(cols)]
        low = jnp.dot(
            jnp.concatenate(kept, axis=1), weights, preferred_element_type=F32
        ).astype(BF16)
        for p in range(pieces):
            outs[p][i % half] = low[:, p * width : (p + 1) * width]
        for k in range(n_fac):
            factor = jnp.where(flags[s * n_fac + k] > 0, factors[k][s], zero)
            added = transposed_dot(*((low, factor) if k else (factor, low)))
            sums[2 * k] += added[:, : tile // 2]
            sums[2 * k + 1] += added[:, tile // 2 :]

    lax.fori_loop(0, half, functools.partial(step, outs=outs[:pieces]), None)
    lax.fori_loop(half, n, functools.partial(step, outs=outs[pieces:]), None)


def products(pieces, ids, marks, flags, ancestor, column, factors):
    n, cols, tile, _ = ancestor.shape
    n_fac = len(factors)
    out = jax.ShapeDtypeStruct((n // 2, tile, tile // pieces), BF16)
    shapes = (out,) * (2 * pieces) + (jax.ShapeDtypeStruct((2 * n_fac, tile, tile // 2), F32),)
    memory = [pltpu.SMEM] * 3 + [pltpu.HBM] + [pltpu.VMEM] * (1 + n_fac)
    *outs, sums = pl.pallas_call(
        functools.partial(product_kernel, n_fac, pieces),
        out_shape=shapes,
        in_specs=[pl.BlockSpec(memory_space=space) for space in memory],
        out_specs=[pl.BlockSpec(memory_space=pltpu.VMEM)] * len(shapes),
        scratch_shapes=[
            pltpu.VMEM((n, cols, tile, tile), BF16),
            pltpu.SemaphoreType.DMA((n,)),
        ],
        compiler_params=pltpu.CompilerParams(vmem_limit_bytes=40 << 20),
        cost_estimate=pl.CostEstimate(
            flops=2 * n * (cols + n_fac) * tile**3,
            bytes_accessed=2 * n * (cols + n_fac + 1) * tile**2,
            transcendentals=0,
        ),
    )(ids, marks, flags, ancestor, column, *factors)
    return outs[:pieces], outs[pieces:], sums


def after(array, *earlier):
    return lax.optimization_barrier((array, *earlier))[0]


def shards(
    ancestor,
    tile_mask,
    member_one,
    member_two,
    factor_one,
    factor_two,
    link_block,
    inverse_one,
    inverse_two,
):
    nrow, ncol = lax.axis_size("row"), lax.axis_size("col")
    row, col = lax.axis_index("row"), lax.axis_index("col")
    rows, cols, tile = ancestor.shape[0], ancestor.shape[1], ancestor.shape[-1]
    group = ncol // nrow
    bits, row_bits = ncol.bit_length() - 1, nrow.bit_length() - 1
    owner = col // group
    at = lambda r, c: r * ncol + c
    everyone = [(r, c) for r in range(nrow) for c in range(ncol)]

    def over_chips(factor, *earlier):
        have = piece = lax.dynamic_slice_in_dim(factor, col % group * cols, cols, 0)
        for k in range(2, nrow, 2):
            perm = [(at(c // group, c), at((c // group + k) % nrow, c)) for c in range(ncol)]
            got = after(lax.ppermute(piece, BOTH, perm), *earlier)
            have = jnp.where((row - owner) % nrow == k, got, have)
        return have

    def over_cores(have):
        perm = [
            (at(2 * y + c // group % 2, c), at(2 * y + 1 - c // group % 2, c))
            for y in range(nrow // 2)
            for c in range(ncol)
        ]
        return jnp.where((row - owner) % 2 == 0, have, lax.ppermute(have, BOTH, perm))

    def swap(array, bit):
        return lax.ppermute(array, BOTH, [(at(r, c), at(r, c ^ (1 << bit))) for r, c in everyone])

    def swap_rows(array, bit):
        return lax.ppermute(array, BOTH, [(at(r, c), at(r ^ (1 << bit), c)) for r, c in everyone])

    def pick(array, bit, other):
        split = array.reshape(array.shape[0] // 2, 2, *array.shape[1:])
        return lax.dynamic_slice_in_dim(split, (col >> bit & 1) ^ other, 1, 1)[:, 0].astype(F32)

    def merged(keep, got, bit, other):
        return pick(keep, bit, other) + pick(got, bit, other)

    flags_one = lax.dynamic_slice_in_dim(member_one, row * rows, rows, 0)
    flags_two = lax.dynamic_slice_in_dim(member_two, row * rows, rows, 0)
    marks = [
        (tile_mask * lax.dynamic_slice_in_dim(m, col * cols, cols, 0)[None]).reshape(-1)
        for m in (member_one, member_two)
    ]
    flags = [jnp.stack([flags_one, flags_one * flags_two], 1).reshape(-1), flags_two]
    ids = jnp.arange(rows // 2, dtype=jnp.int32) * 2
    ids = jnp.concatenate([ids + (1 - col % 2), ids + col % 2])

    column = over_cores(over_chips(factor_one, *marks, *flags, ids))
    (away,), (keep_one,), sums_one = products(
        1, ids, marks[0], flags[0], ancestor, column, (factor_one, factor_two)
    )
    one = [swap(away, 0)]
    column = over_cores(over_chips(factor_two, keep_one))
    (away_a, away_b), (keep_a, keep_b), sums_two = products(
        2, ids, marks[1], flags[1], ancestor, column, (factor_two,)
    )

    sums = jnp.concatenate([sums_one, sums_two])
    shape = sums.shape
    part = sums.reshape(-1, shape[-1])
    for bit in range(row_bits):
        half = part.shape[0] // 2
        mine = row >> bit & 1
        if bit == row_bits - 1:
            part = after(part, one[0])
        got = swap_rows(lax.dynamic_slice_in_dim(part, (1 - mine) * half, half, 0).astype(BF16), bit)
        part = lax.dynamic_slice_in_dim(part, mine * half, half, 0) + got.astype(F32)
    part = part.astype(BF16)

    b = []
    for bit in range(bits):
        if bit:
            away = merged(keep_one, one[-1], bit, 1).astype(BF16)
            keep_one = merged(keep_one, one[-1], bit, 0)
            one.append(swap(after(away, b[bit - 2]) if bit > 1 else away, bit))
            away_a = merged(keep_a, got_a, bit, 1).astype(BF16)
            keep_a = merged(keep_a, got_a, bit, 0)
            away_b = merged(keep_b, b[-1], bit, 1).astype(BF16)
            keep_b = merged(keep_b, b[-1], bit, 0)
        else:
            away_b = after(away_b, one[0])
        message = jnp.concatenate([away_a.reshape(-1, tile // 2), part])
        message = swap(after(message, one[bit]), bit)
        b.append(swap(away_b, bit))
        got_a = message[: -part.shape[0]].reshape(away_a.shape)
        part = (part.astype(F32) + message[-part.shape[0] :].astype(F32)).astype(BF16)

    for bit in reversed(range(row_bits)):
        got = swap_rows(after(part, b[-1] if bit == 0 else b[-2]), bit)
        low = (row >> bit & 1) == 0
        part = jnp.concatenate([jnp.where(low, part, got), jnp.where(low, got, part)])

    column_one, column_two = small_kernel(
        column_kernel,
        2,
        1,
        tile,
        (
            member_one,
            member_two,
            (row * rows + col)[None],
            link_block,
            *(a[0] for a in (keep_one, one[-1], keep_a, got_a, keep_b, b[-1])),
        ),
        3,
    )
    diag_one, cross_block, diag_two = small_kernel(
        diagonal_kernel, 3, 3, tile, (part.reshape(shape), link_block, inverse_one, inverse_two)
    )
    return (column_one[None], column_two[None], diag_one, cross_block, diag_two)


def solution(mesh):
    in_specs = (
        P("row", "col", None, None),
        P("row", "col"),
        P(),
        P(),
        P("row", None, None),
        P("row", None, None),
        P(),
        P(),
        P(),
    )
    out_specs = (P(("row", "col"), None, None), P(("row", "col"), None, None), P(), P(), P())
    return jax.shard_map(shards, mesh=mesh, in_specs=in_specs, out_specs=out_specs, check_vma=False)
```

time: 98.8 us -> 95 us (0.962)
  waiting for transfers between devices: 42.4 us -> 32.4 us
  starting transfers between devices: 19.6 us -> 26.3 us
  local copies, waits for them, and re-layouts: 9.1 us -> 11 us
  other arithmetic: 9.41 us -> 8.31 us
    ppermute x17, waiting for transfers between devices: 42.4 us -> 32.4 us  [the longest x9 22 us: swap(): lax.ppermute(array, BOTH, [(at(r, c), at(r, c ^ 1 << bit)) for r, c in ev...]
    ppermute x17, starting transfers between devices: 19.6 us -> 26.3 us  [the longest x9 12.4 us: swap(): lax.ppermute(array, BOTH, [(at(r, c), at(r, c ^ 1 << bit)) for r, c in ev...]
    unnamed x16 -> x14, local copies, waits for them, and re-layouts: 2.87 us -> 5.18 us
    another operation x1 -> x0, other arithmetic: 1.85 us -> none  [shards(): jnp.stack([lax.dynamic_index_in_dim(m, col, keepdims=False) for m in (fla...]
    dynamic_slice x4 -> x2, local copies, waits for them, and re-layouts: 4.25 us -> 3.11 us  [over_chips(): have = piece = lax.dynamic_slice_in_dim(factor, col % group * cols, cols, 0)]
    convert_element_type x7 -> x8, other arithmetic: 2.68 us -> 2.66 us  [the longest x2 1.77 us: shards(): away = merged(keep_one, one[-1], bit, 1).astype(BF16)]
  transfers between devices with their start and end apart: 17 -> 17, of which waited for: 10 -> 10; matrix products, arithmetic and copies ran while one was open for 14% -> 11% of each run, Pallas kernels for 14% -> 14%
where the time goes in v2:
time: 95 us; the launch traced here: 94.4 us
  waiting for transfers between devices  32.4 us (34%)
  starting transfers between devices  26.3 us (28%)
  Pallas kernels  15.5 us (16%)
  local copies, waits for them, and re-layouts  11 us (12%)
  other arithmetic  8.31 us (9%)
  between operations  0.96 us (1%)
    ppermute x9, waiting for transfers between devices, swap(): lax.ppermute(array, BOTH, [(at(r, c), at(r, c ^ 1 << bit)) for r, c in ev...  22 us
    ppermute x9, starting transfers between devices, swap(): lax.ppermute(array, BOTH, [(at(r, c), at(r, c ^ 1 << bit)) for r, c in ev...  12.4 us
    pallas_call x2, Pallas kernels, products(): pl.pallas_call(functools.partial(product_kernel, n_fac, pieces), out_shap...  11.2 us
    ppermute x2, starting transfers between devices, over_chips(): got = after(lax.ppermute(piece, BOTH, perm), *earlier)  10.1 us
    ppermute x4, waiting for transfers between devices, swap_rows(): lax.ppermute(array, BOTH, [(at(r, c), at(r ^ 1 << bit, c)) for r, c in ev...  7.24 us
    unnamed x14, local copies, waits for them, and re-layouts  5.18 us
    pallas_call x2, Pallas kernels, small_kernel(): pl.pallas_call(body, out_shape=(jax.ShapeDtypeStruct((tile, tile), BF16),...  4.29 us
    dynamic_slice x2, local copies, waits for them, and re-layouts, over_chips(): have = piece = lax.dynamic_slice_in_dim(factor, col % group * cols, cols, 0)  3.11 us
  transfers between devices with their start and end apart: 17, of which 10 were waited for; matrix products, arithmetic and copies ran while one was open for 11% of the time, Pallas kernels for 14%

profile of v2, /device:TPU:0, one launch (start us, length us, event | category | flops | bytes accessed | tf_op | source)
XLA Modules:
  0.0 94.4 jit_solution(14921786734258368580)
XLA Ops:
  0.7 1.2 %constant_dynamic-slice_fusion.1 = bf16[4,256,256]{2,1,0:T(8,128)(2,1)S(1)} fusion(bf16[8,256,256]{2,1,0:T(8,128)(2,1)} %refs_0_.2, s32[]{:T(128)S(6)} %select_n.139), kind=kLoop, calls=%fused_computation.41 | loop fusion | bytes 1048580 | tf_op jit(solution)/shard_map/dynamic_slice | solution.py:138
  1.9 4.9 %collective-permute-start = (bf16[4,256,256]{2,1,0:T(8,128)(2,1)S(1)}, bf16[4,256,256]{2,1,0:T(8,128)(2,1)S(1)}, u32[]{:S(2)}, u32[]{:S(2)}) collective-permute-start(bf16[4,256,256]{2,1,0:T(8,128)(2,1)S(1)} %constant_dynamic-slice_fusion.1), channel_id=1, source_target_pairs={{0,16},{1,17},{10,26},{11,27},{20,4},{21,5},{30,14},{31,15}} | collective-permute-start | bytes 1572872 | tf_op jit(solution)/shard_map/ppermute | solution.py:141
  10.4 3.1 %collective-permute-done = bf16[4,256,256]{2,1,0:T(8,128)(2,1)S(1)} collective-permute-done((bf16[4,256,256]{2,1,0:T(8,128)(2,1)S(1)}, bf16[4,256,256]{2,1,0:T(8,128)(2,1)S(1)}, u32[]{:S(2)}, u32[]{:S(2)}) %collective-permute-start) | collective-permute-done | bytes 524320 | tf_op jit(solution)/shard_map/ppermute | solution.py:141
  13.5 1.1 %broadcast_select_fusion.1 = bf16[4,256,256]{2,1,0:T(8,128)(2,1)S(1)} fusion(bf16[4,256,256]{2,1,0:T(8,128)(2,1)S(1)} %collective-permute-done, pred[]{:T(512)S(6)} %eq.24, bf16[8,256,256]{2,1,0:T(8,128)(2,1)} %refs_0_.2, s32[]{:T(128)S(6)} %select_n.139), kind=kLoop, calls=%fused_computation.4 | loop fusion | flops 262144 | bytes 1572869 | tf_op jit(solution)/shard_map/jit(_where)/select_n | solution.py:142
  14.6 1.3 %collective-permute-start.1 = (bf16[4,256,256]{2,1,0:T(8,128)(2,1)S(1)}, bf16[4,256,256]{2,1,0:T(8,128)(2,1)S(1)}, u32[]{:S(2)}, u32[]{:S(2)}) collective-permute-start(bf16[4,256,256]{2,1,0:T(8,128)(2,1)S(1)} %broadcast_select_fusion.1), channel_id=1, source_target_pairs={{0,8},{1,9},{10,2},{11,3},{4,12},{5,13},{14,6},{15,7},{16,24},{17,... | collective-permute-start | bytes 1572872 | tf_op jit(solution)/shard_map/ppermute | solution.py:151
  15.9 1.9 %constant_dynamic-slice_fusion = bf16[4,256,256]{2,1,0:T(8,128)(2,1)} fusion(bf16[8,256,256]{2,1,0:T(8,128)(2,1)} %refs_0_.3, s32[]{:T(128)S(6)} %select_n.139), kind=kLoop, calls=%fused_computation.40 | loop fusion | bytes 1048580 | tf_op jit(solution)/shard_map/dynamic_slice | solution.py:138
  17.8 5.2 %collective-permute-start.4 = (bf16[4,256,256]{2,1,0:T(8,128)(2,1)}, bf16[4,256,256]{2,1,0:T(8,128)(2,1)}, u32[]{:S(2)}, u32[]{:S(2)}) collective-permute-start(bf16[4,256,256]{2,1,0:T(8,128)(2,1)} %constant_dynamic-slice_fusion), channel_id=1, source_target_pairs={{0,16},{1,17},{10,26},{11,27},{20,4},{21,5},{30,14},{31,15}} | collective-permute-start | bytes 1572872 | tf_op jit(solution)/shard_map/ppermute | solution.py:141
  23.0 2.2 %copy-done = bf16[8,4,256,256]{3,2,1,0:T(8,128)(2,1)S(1)} copy-done((bf16[8,4,256,256]{3,2,1,0:T(8,128)(2,1)S(1)}, bf16[8,4,256,256]{3,2,1,0:T(8,128)(2,1)}, u32[]{:S(2)}) %copy-start) | copy-done | bytes 4194328
  25.2 6.0 %shard_map.128 = (bf16[4,256,256]{2,1,0:T(8,128)(2,1)S(1)}, bf16[4,256,256]{2,1,0:T(8,128)(2,1)S(1)}, f32[4,256,128]{2,1,0:T(8,128)S(1)}) custom-call(s32[8]{0:T(128)S(1)} %pad_add_fusion.1.ids, s32[32]{0:T(128)S(1)} %reshape.175.marks, s32[16]{0:T(128)S(1)} %reshape.176.flags, bf16[8,4,256,256]{3,2,1,0:T(8,128)(2,1)S(1)} %copy-done, ...), custom_call_target="tpu_custom_call" | custom-call | flops 1610612736 | bytes 7340032 | tf_op jit(solution)/shard_map/pallas_call | solution.py:94
  31.2 0.8 copy-done.4
  32.1 1.3 %collective-permute-start.5 = (bf16[4,256,256]{2,1,0:T(8,128)(2,1)S(1)}, bf16[4,256,256]{2,1,0:T(8,128)(2,1)S(1)}, u32[]{:S(2)}, u32[]{:S(2)}) collective-permute-start(bf16[4,256,256]{2,1,0:T(8,128)(2,1)S(1)} %broadcast_select_fusion), channel_id=1, source_target_pairs={{0,8},{1,9},{10,2},{11,3},{4,12},{5,13},{14,6},{15,7},{16,24},{17,... | collective-permute-start | bytes 1572872 | tf_op jit(solution)/shard_map/ppermute | solution.py:151
  33.4 1.6 %collective-permute-start.2 = (bf16[4,256,256]{2,1,0:T(8,128)(2,1)}, bf16[4,256,256]{2,1,0:T(8,128)(2,1)}, u32[]{:S(2)}, u32[]{:S(2)}) collective-permute-start(bf16[4,256,256]{2,1,0:T(8,128)(2,1)} %copy-done.4), channel_id=1, source_target_pairs={{0,1},{1,0},{2,3},{3,2},{4,5},{5,4},{6,7},{7,6},{8,9},{9,8},{10,11... | collective-permute-start | bytes 1572872 | tf_op jit(solution)/shard_map/ppermute | solution.py:154
  35.0 2.2 %copy-done.1 = bf16[8,4,256,256]{3,2,1,0:T(8,128)(2,1)S(1)} copy-done((bf16[8,4,256,256]{3,2,1,0:T(8,128)(2,1)S(1)}, bf16[8,4,256,256]{3,2,1,0:T(8,128)(2,1)}, u32[]{:S(2)}) %copy-start.1) | copy-done | bytes 4194328
  37.2 5.2 %shard_map.129 = (bf16[4,256,128]{2,1,0:T(8,128)(2,1)S(1)}, bf16[4,256,128]{2,1,0:T(8,128)(2,1)S(1)}, bf16[4,256,128]{2,1,0:T(8,128)(2,1)S(1)}, bf16[4,256,128]{2,1,0:T(8,128)(2,1)S(1)}, f32[2,256,128]{2,1,0:T(8,128)S(1)}) custom-call(s32[8]{0:T(128)S(1)} %pad_add_fusion.1.ids, s32[32]{0:T(128)S(1)} %reshape.177.marks, s32[8]{0:T(128)S(1)} %get-tuple-element.52.flags, ...), custom_call_target="tpu_custom_call" | custom-call | flops 1342177280 | bytes 6291456 | tf_op jit(solution)/shard_map/pallas_call | solution.py:94
  42.9 1.1 %collective-permute-done.8 = bf16[768,128]{1,0:T(8,128)(2,1)S(1)} collective-permute-done((bf16[768,128]{1,0:T(8,128)(2,1)S(1)}, bf16[768,128]{1,0:T(8,128)(2,1)S(1)}, u32[]{:S(2)}, u32[]{:S(2)}) %collective-permute-start.8) | collective-permute-done | bytes 196640 | tf_op jit(solution)/shard_map/ppermute | solution.py:157
  44.1 0.8 collective-permute-start.9
  44.9 4.2 %collective-permute-done.9 = bf16[384,128]{1,0:T(8,128)(2,1)S(1)} collective-permute-done((bf16[384,128]{1,0:T(8,128)(2,1)S(1)}, bf16[384,128]{1,0:T(8,128)(2,1)S(1)}, u32[]{:S(2)}, u32[]{:S(2)}) %collective-permute-start.9) | collective-permute-done | bytes 98336 | tf_op jit(solution)/shard_map/ppermute | solution.py:157
  49.2 1.6 %collective-permute-start.10 = (bf16[1408,128]{1,0:T(8,128)(2,1)S(1)}, bf16[1408,128]{1,0:T(8,128)(2,1)S(1)}, u32[]{:S(2)}, u32[]{:S(2)}) collective-permute-start(bf16[1408,128]{1,0:T(8,128)(2,1)S(1)} %pad_maximum_fusion.2), channel_id=1, source_target_pairs={{0,1},{1,0},{2,3},{3,2},{4,5},{5,4},{6,7},{7,6},{8,9},{9,8},{10,11... | collective-permute-start | bytes 1081352 | tf_op jit(solution)/shard_map/ppermute | solution.py:154
  50.8 1.0 %fusion = bf16[2,256,256]{2,1,0:T(8,128)(2,1)S(1)} fusion(bf16[2,2,256,256]{3,2,1,0:T(8,128)(2,1)} %bitcast.4, s32[]{:T(128)S(6)} %select_n.144, bf16[2,2,256,256]{3,2,1,0:T(8,128)(2,1)S(1)} %bitcast.56), kind=kLoop, calls=%fused_computation.11 | loop fusion | flops 524288 | bytes 786436 | tf_op jit(solution)/shard_map/convert_element_type | solution.py:201
  52.5 8.2 %collective-permute-done.10 = bf16[1408,128]{1,0:T(8,128)(2,1)S(1)} collective-permute-done((bf16[1408,128]{1,0:T(8,128)(2,1)S(1)}, bf16[1408,128]{1,0:T(8,128)(2,1)S(1)}, u32[]{:S(2)}, u32[]{:S(2)}) %collective-permute-start.10) | collective-permute-done | bytes 360480 | tf_op jit(solution)/shard_map/ppermute | solution.py:154
  60.9 1.0 %convert_add_fusion = f32[2,1,256,256]{3,2,1,0:T(8,128)S(1)} fusion(bf16[2,2,256,256]{3,2,1,0:T(8,128)(2,1)} %bitcast.4, s32[]{:T(128)S(6)} %select_n.142, bf16[2,2,256,256]{3,2,1,0:T(8,128)(2,1)S(1)} %bitcast.57), kind=kLoop, calls=%fused_computation.2 | loop fusion | flops 393216 | bytes 1048580 | tf_op jit(solution)/shard_map/add | solution.py:164
  62.7 2.0 %collective-permute-done.6 = bf16[4,256,128]{2,1,0:T(8,128)(2,1)S(1)} collective-permute-done((bf16[4,256,128]{2,1,0:T(8,128)(2,1)S(1)}, bf16[4,256,128]{2,1,0:T(8,128)(2,1)S(1)}, u32[]{:S(2)}, u32[]{:S(2)}) %collective-permute-start.6) | collective-permute-done | bytes 262176 | tf_op jit(solution)/shard_map/ppermute | solution.py:154
  64.7 1.6 %collective-permute-start.7 = (bf16[1,256,256]{2,1,0:T(8,128)(2,1)S(1)}, bf16[1,256,256]{2,1,0:T(8,128)(2,1)S(1)}, u32[]{:S(2)}, u32[]{:S(2)}) collective-permute-start(bf16[1,256,256]{2,1,0:T(8,128)(2,1)S(1)} %get-tuple-element.34), channel_id=1, source_target_pairs={{0,4},{1,5},{2,6},{3,7},{4,0},{5,1},{6,2},{7,3},{8,12},{9,13},{10,... | collective-permute-start | bytes 393224 | tf_op jit(solution)/shard_map/ppermute | solution.py:154
  67.8 4.4 %collective-permute-done.7 = bf16[1,256,256]{2,1,0:T(8,128)(2,1)S(1)} collective-permute-done((bf16[1,256,256]{2,1,0:T(8,128)(2,1)S(1)}, bf16[1,256,256]{2,1,0:T(8,128)(2,1)S(1)}, u32[]{:S(2)}, u32[]{:S(2)}) %collective-permute-start.7) | collective-permute-done | bytes 131104 | tf_op jit(solution)/shard_map/ppermute | solution.py:154
  72.3 4.7 %collective-permute-start.13 = (bf16[2,256,128]{2,1,0:T(8,128)(2,1)S(1)}, bf16[2,256,128]{2,1,0:T(8,128)(2,1)S(1)}, u32[]{:S(2)}, u32[]{:S(2)}) collective-permute-start(bf16[2,256,128]{2,1,0:T(8,128)(2,1)S(1)} %fusion.3), channel_id=1, source_target_pairs={{0,2},{1,3},{2,0},{3,1},{4,6},{5,7},{6,4},{7,5},{8,10},{9,11},{10,... | collective-permute-start | bytes 393224 | tf_op jit(solution)/shard_map/ppermute | solution.py:154
  77.1 4.8 %collective-permute-done.12 = bf16[640,128]{1,0:T(8,128)(2,1)S(1)} collective-permute-done((bf16[640,128]{1,0:T(8,128)(2,1)S(1)}, bf16[640,128]{1,0:T(8,128)(2,1)S(1)}, u32[]{:S(2)}, u32[]{:S(2)}) %collective-permute-start.12) | collective-permute-done | bytes 163872 | tf_op jit(solution)/shard_map/ppermute | solution.py:154
  82.7 2.0 %collective-permute-start.14 = (bf16[1,256,128]{2,1,0:T(8,128)(2,1)S(1)}, bf16[1,256,128]{2,1,0:T(8,128)(2,1)S(1)}, u32[]{:S(2)}, u32[]{:S(2)}) collective-permute-start(bf16[1,256,128]{2,1,0:T(8,128)(2,1)S(1)} %get-tuple-element.59), channel_id=1, source_target_pairs={{0,4},{1,5},{2,6},{3,7},{4,0},{5,1},{6,2},{7,3},{8,12},{9,13},{10,... | collective-permute-start | bytes 196616 | tf_op jit(solution)/shard_map/ppermute | solution.py:154
  84.8 1.9 %collective-permute-done.15 = bf16[384,128]{1,0:T(8,128)(2,1)S(1)} collective-permute-done((bf16[384,128]{1,0:T(8,128)(2,1)S(1)}, bf16[384,128]{1,0:T(8,128)(2,1)S(1)}, u32[]{:S(2)}, u32[]{:S(2)}) %collective-permute-start.15) | collective-permute-done | bytes 98336 | tf_op jit(solution)/shard_map/ppermute | solution.py:157
  86.7 1.9 %collective-permute-done.14 = bf16[1,256,128]{2,1,0:T(8,128)(2,1)S(1)} collective-permute-done((bf16[1,256,128]{2,1,0:T(8,128)(2,1)S(1)}, bf16[1,256,128]{2,1,0:T(8,128)(2,1)S(1)}, u32[]{:S(2)}, u32[]{:S(2)}) %collective-permute-start.14) | collective-permute-done | bytes 65568 | tf_op jit(solution)/shard_map/ppermute | solution.py:154
  89.3 2.0 %shard_map.130 = (bf16[256,256]{1,0:T(8,128)(2,1)}, bf16[256,256]{1,0:T(8,128)(2,1)}) custom-call(s32[32]{0:T(128)} %first.1, s32[32]{0:T(128)} %second.1, s32[1]{0:T(128)} %bitcast.place, bf16[256,256]{1,0:T(8,128)(2,1)} %link.3, f32[256,256]{1,0:T(8,128)} %get-tuple-element.54.refs_0_, bf16[256,256]{1,0:T(8,128)(2,1)} %bitcast.70, ...), custom_call_target="tpu_custom_call" | custom-call | flops 33554432 | bytes 2621440 | tf_op jit(solution)/shard_map/pallas_call | solution.py:44
  91.4 0.8 pad_maximum_fusion.1
  92.1 2.3 %shard_map.131 = (bf16[256,256]{1,0:T(8,128)(2,1)}, bf16[256,256]{1,0:T(8,128)(2,1)}, bf16[256,256]{1,0:T(8,128)(2,1)}) custom-call(bf16[6,256,128]{2,1,0:T(8,128)(2,1)} %bitcast.64, bf16[256,256]{1,0:T(8,128)(2,1)} %link.3, f32[256,256]{1,0:T(8,128)} %inverse_one.1, f32[256,256]{1,0:T(8,128)} %inverse_two.1), custom_call_target="tpu_custom_call" | custom-call | flops 100663296 | bytes 1048576 | tf_op jit(solution)/shard_map/pallas_call | solution.py:44
  (65 shorter events, 9.1 us)
Async XLA Ops:
  0.6 22.4 %copy-start.3 = (bf16[8,256,256]{2,1,0:T(8,128)(2,1)S(1)}, bf16[8,256,256]{2,1,0:T(8,128)(2,1)}, u32[]{:S(2)}) copy-start(bf16[8,256,256]{2,1,0:T(8,128)(2,1)} %refs_0_.2) | copy-start | bytes 3145732
  0.6 22.4 %copy-start.2 = (bf16[8,256,256]{2,1,0:T(8,128)(2,1)S(1)}, bf16[8,256,256]{2,1,0:T(8,128)(2,1)}, u32[]{:S(2)}) copy-start(bf16[8,256,256]{2,1,0:T(8,128)(2,1)} %refs_0_.3) | copy-start | bytes 3145732
  1.9 11.6 %collective-permute-start = (bf16[4,256,256]{2,1,0:T(8,128)(2,1)S(1)}, bf16[4,256,256]{2,1,0:T(8,128)(2,1)S(1)}, u32[]{:S(2)}, u32[]{:S(2)}) collective-permute-start(bf16[4,256,256]{2,1,0:T(8,128)(2,1)S(1)} %constant_dynamic-slice_fusion.1), channel_id=1, source_target_pairs={{0,16},{1,17},{10,26},{11,27},{20,4},{21,5},{30,14},{31,15}} | collective-permute-start | bytes 1572872 | tf_op jit(solution)/shard_map/ppermute | solution.py:141
  14.6 8.4 %collective-permute-start.1 = (bf16[4,256,256]{2,1,0:T(8,128)(2,1)S(1)}, bf16[4,256,256]{2,1,0:T(8,128)(2,1)S(1)}, u32[]{:S(2)}, u32[]{:S(2)}) collective-permute-start(bf16[4,256,256]{2,1,0:T(8,128)(2,1)S(1)} %broadcast_select_fusion.1), channel_id=1, source_target_pairs={{0,8},{1,9},{10,2},{11,3},{4,12},{5,13},{14,6},{15,7},{16,24},{17,... | collective-permute-start | bytes 1572872 | tf_op jit(solution)/shard_map/ppermute | solution.py:151
  17.8 14.2 %collective-permute-start.4 = (bf16[4,256,256]{2,1,0:T(8,128)(2,1)}, bf16[4,256,256]{2,1,0:T(8,128)(2,1)}, u32[]{:S(2)}, u32[]{:S(2)}) collective-permute-start(bf16[4,256,256]{2,1,0:T(8,128)(2,1)} %constant_dynamic-slice_fusion), channel_id=1, source_target_pairs={{0,16},{1,17},{10,26},{11,27},{20,4},{21,5},{30,14},{31,15}} | collective-permute-start | bytes 1572872 | tf_op jit(solution)/shard_map/ppermute | solution.py:141
  23.0 2.2 %copy-start = (bf16[8,4,256,256]{3,2,1,0:T(8,128)(2,1)S(1)}, bf16[8,4,256,256]{3,2,1,0:T(8,128)(2,1)}, u32[]{:S(2)}) copy-start(bf16[8,4,256,256]{3,2,1,0:T(8,128)(2,1)} %anc.3) | copy-start | bytes 12582916
  31.2 0.8 copy-start.4
  32.1 2.9 %collective-permute-start.5 = (bf16[4,256,256]{2,1,0:T(8,128)(2,1)S(1)}, bf16[4,256,256]{2,1,0:T(8,128)(2,1)S(1)}, u32[]{:S(2)}, u32[]{:S(2)}) collective-permute-start(bf16[4,256,256]{2,1,0:T(8,128)(2,1)S(1)} %broadcast_select_fusion), channel_id=1, source_target_pairs={{0,8},{1,9},{10,2},{11,3},{4,12},{5,13},{14,6},{15,7},{16,24},{17,... | collective-permute-start | bytes 1572872 | tf_op jit(solution)/shard_map/ppermute | solution.py:151
  33.4 10.7 %collective-permute-start.2 = (bf16[4,256,256]{2,1,0:T(8,128)(2,1)}, bf16[4,256,256]{2,1,0:T(8,128)(2,1)}, u32[]{:S(2)}, u32[]{:S(2)}) collective-permute-start(bf16[4,256,256]{2,1,0:T(8,128)(2,1)} %copy-done.4), channel_id=1, source_target_pairs={{0,1},{1,0},{2,3},{3,2},{4,5},{5,4},{6,7},{7,6},{8,9},{9,8},{10,11... | collective-permute-start | bytes 1572872 | tf_op jit(solution)/shard_map/ppermute | solution.py:154
  35.0 2.2 %copy-start.1 = (bf16[8,4,256,256]{3,2,1,0:T(8,128)(2,1)S(1)}, bf16[8,4,256,256]{3,2,1,0:T(8,128)(2,1)}, u32[]{:S(2)}) copy-start(bf16[8,4,256,256]{3,2,1,0:T(8,128)(2,1)} %anc.3) | copy-start | bytes 12582916
  42.5 1.5 %collective-permute-start.8 = (bf16[768,128]{1,0:T(8,128)(2,1)S(1)}, bf16[768,128]{1,0:T(8,128)(2,1)S(1)}, u32[]{:S(2)}, u32[]{:S(2)}) collective-permute-start(bf16[768,128]{1,0:T(8,128)(2,1)S(1)} %dynamic-slice_convert_fusion), channel_id=1, source_target_pairs={{0,8},{1,9},{2,10},{3,11},{4,12},{5,13},{6,14},{7,15},{8,0},{9,1},... | collective-permute-start | bytes 589832 | tf_op jit(solution)/shard_map/ppermute | solution.py:157
  44.1 5.1 %collective-permute-start.9 = (bf16[384,128]{1,0:T(8,128)(2,1)S(1)}, bf16[384,128]{1,0:T(8,128)(2,1)S(1)}, u32[]{:S(2)}, u32[]{:S(2)}) collective-permute-start(bf16[384,128]{1,0:T(8,128)(2,1)S(1)} %dynamic-slice_convert_fusion.1), channel_id=1, source_target_pairs={{0,16},{1,17},{2,18},{3,19},{4,20},{5,21},{6,22},{7,23},{8,24},{9,... | collective-permute-start | bytes 294920 | tf_op jit(solution)/shard_map/ppermute | solution.py:157
  49.2 11.4 %collective-permute-start.10 = (bf16[1408,128]{1,0:T(8,128)(2,1)S(1)}, bf16[1408,128]{1,0:T(8,128)(2,1)S(1)}, u32[]{:S(2)}, u32[]{:S(2)}) collective-permute-start(bf16[1408,128]{1,0:T(8,128)(2,1)S(1)} %pad_maximum_fusion.2), channel_id=1, source_target_pairs={{0,1},{1,0},{2,3},{3,2},{4,5},{5,4},{6,7},{7,6},{8,9},{9,8},{10,11... | collective-permute-start | bytes 1081352 | tf_op jit(solution)/shard_map/ppermute | solution.py:154
  51.8 9.0 %collective-permute-start.3 = (bf16[2,256,256]{2,1,0:T(8,128)(2,1)S(1)}, bf16[2,256,256]{2,1,0:T(8,128)(2,1)S(1)}, u32[]{:S(2)}, u32[]{:S(2)}) collective-permute-start(bf16[2,256,256]{2,1,0:T(8,128)(2,1)S(1)} %fusion), channel_id=1, source_target_pairs={{0,2},{1,3},{2,0},{3,1},{4,6},{5,7},{6,4},{7,5},{8,10},{9,11},{10,... | collective-permute-start | bytes 786440 | tf_op jit(solution)/shard_map/ppermute | solution.py:154
  51.9 12.8 %collective-permute-start.6 = (bf16[4,256,128]{2,1,0:T(8,128)(2,1)S(1)}, bf16[4,256,128]{2,1,0:T(8,128)(2,1)S(1)}, u32[]{:S(2)}, u32[]{:S(2)}) collective-permute-start(bf16[4,256,128]{2,1,0:T(8,128)(2,1)S(1)} %get-tuple-element.33), channel_id=1, source_target_pairs={{0,1},{1,0},{2,3},{3,2},{4,5},{5,4},{6,7},{7,6},{8,9},{9,8},{10,11... | collective-permute-start | bytes 786440 | tf_op jit(solution)/shard_map/ppermute | solution.py:154
  60.8 6.2 %collective-permute-start.11 = (bf16[896,128]{1,0:T(8,128)(2,1)S(1)}, bf16[896,128]{1,0:T(8,128)(2,1)S(1)}, u32[]{:S(2)}, u32[]{:S(2)}) collective-permute-start(bf16[896,128]{1,0:T(8,128)(2,1)S(1)} %pad_maximum_fusion.3), channel_id=1, source_target_pairs={{0,2},{1,3},{2,0},{3,1},{4,6},{5,7},{6,4},{7,5},{8,10},{9,11},{10,... | collective-permute-start | bytes 688136 | tf_op jit(solution)/shard_map/ppermute | solution.py:154
  64.7 7.5 %collective-permute-start.7 = (bf16[1,256,256]{2,1,0:T(8,128)(2,1)S(1)}, bf16[1,256,256]{2,1,0:T(8,128)(2,1)S(1)}, u32[]{:S(2)}, u32[]{:S(2)}) collective-permute-start(bf16[1,256,256]{2,1,0:T(8,128)(2,1)S(1)} %get-tuple-element.34), channel_id=1, source_target_pairs={{0,4},{1,5},{2,6},{3,7},{4,0},{5,1},{6,2},{7,3},{8,12},{9,13},{10,... | collective-permute-start | bytes 393224 | tf_op jit(solution)/shard_map/ppermute | solution.py:154
  72.2 17.1 %copy-start.5 = (bf16[1,256,256]{2,1,0:T(8,128)(2,1)}, bf16[1,256,256]{2,1,0:T(8,128)(2,1)S(1)}, u32[]{:S(2)}) copy-start(bf16[1,256,256]{2,1,0:T(8,128)(2,1)S(1)} %collective-permute-done.7) | copy-start | bytes 393220
  72.2 9.7 %collective-permute-start.12 = (bf16[640,128]{1,0:T(8,128)(2,1)S(1)}, bf16[640,128]{1,0:T(8,128)(2,1)S(1)}, u32[]{:S(2)}, u32[]{:S(2)}) collective-permute-start(bf16[640,128]{1,0:T(8,128)(2,1)S(1)} %pad_maximum_fusion.5), channel_id=1, source_target_pairs={{0,4},{1,5},{2,6},{3,7},{4,0},{5,1},{6,2},{7,3},{8,12},{9,13},{10,... | collective-permute-start | bytes 491528 | tf_op jit(solution)/shard_map/ppermute | solution.py:154
  72.3 9.6 %collective-permute-start.13 = (bf16[2,256,128]{2,1,0:T(8,128)(2,1)S(1)}, bf16[2,256,128]{2,1,0:T(8,128)(2,1)S(1)}, u32[]{:S(2)}, u32[]{:S(2)}) collective-permute-start(bf16[2,256,128]{2,1,0:T(8,128)(2,1)S(1)} %fusion.3), channel_id=1, source_target_pairs={{0,2},{1,3},{2,0},{3,1},{4,6},{5,7},{6,4},{7,5},{8,10},{9,11},{10,... | collective-permute-start | bytes 393224 | tf_op jit(solution)/shard_map/ppermute | solution.py:154
  82.0 4.7 %collective-permute-start.15 = (bf16[384,128]{1,0:T(8,128)(2,1)S(1)}, bf16[384,128]{1,0:T(8,128)(2,1)S(1)}, u32[]{:S(2)}, u32[]{:S(2)}) collective-permute-start(bf16[384,128]{1,0:T(8,128)(2,1)S(1)} %add_convert_fusion.3), channel_id=1, source_target_pairs={{0,16},{1,17},{2,18},{3,19},{4,20},{5,21},{6,22},{7,23},{8,24},{9,... | collective-permute-start | bytes 294920 | tf_op jit(solution)/shard_map/ppermute | solution.py:157
  82.7 5.9 %collective-permute-start.14 = (bf16[1,256,128]{2,1,0:T(8,128)(2,1)S(1)}, bf16[1,256,128]{2,1,0:T(8,128)(2,1)S(1)}, u32[]{:S(2)}, u32[]{:S(2)}) collective-permute-start(bf16[1,256,128]{2,1,0:T(8,128)(2,1)S(1)} %get-tuple-element.59), channel_id=1, source_target_pairs={{0,4},{1,5},{2,6},{3,7},{4,0},{5,1},{6,2},{7,3},{8,12},{9,13},{10,... | collective-permute-start | bytes 196616 | tf_op jit(solution)/shard_map/ppermute | solution.py:154
  88.6 0.7 copy-start.6
  88.6 2.7 %collective-permute-start.16 = (bf16[768,128]{1,0:T(8,128)(2,1)S(1)}, bf16[768,128]{1,0:T(8,128)(2,1)S(1)}, u32[]{:S(2)}, u32[]{:S(2)}) collective-permute-start(bf16[768,128]{1,0:T(8,128)(2,1)S(1)} %pad_maximum_fusion.4), channel_id=1, source_target_pairs={{0,8},{1,9},{2,10},{3,11},{4,12},{5,13},{6,14},{7,15},{8,0},{9,1},... | collective-permute-start | bytes 589832 | tf_op jit(solution)/shard_map/ppermute | solution.py:157
